TPU v7x, 1024 devices: a whole 8x8x8 slice. The times are simulated.
1024 devices in a mesh: row: 16 (over x_lo, z), col: 64 (over y, x_hi, core).
Axes of the slice: x: 8 (x_hi: 4, x_lo: 2; x = x_hi * 2 + x_lo), y: 8, z: 8, core: 2. Of those that a mesh axis runs over, the one named last changes fastest.
Arguments:
- base_weights: float32 [32, 7168, 2048], P(None, 'col', 'row'), may hold values from -6 to 6
- factor_down: float32 [32, 7168, 128], P(None, 'col', 'row'), may hold values from -6 to 6
- factor_up: float32 [32, 128, 2048], P(None, 'col', 'row'), may hold values from -0.5 to 0.5
- presence: int32 [2, 16], replicated, may hold values 0 or 1
- serving_order: int32 [32], replicated, may hold values from 0 to 31, each once
Outputs:
- served: bfloat16 [32, 7168, 2048], P('row', 'col')
Inputs may be any that keep to these rules, and one draw needn't show every extreme that they name: `serving_order`: each value appears exactly once.
All inputs are finite; a program needn't handle non-finite values.
Results may differ from a plain program's by a relative error of at most 0.00105.
Values may be sent and summed in bfloat16 or wider, within the bound.
No kernel may reach another device: no remote copies, remote signals or barrier semaphores. Data moves between devices by JAX's collectives and lax.ppermute only.
A program may use at most 32 MiB of HBM per device.

v0:
```python
import jax
import jax.numpy as jnp
from jax import lax
from jax.sharding import PartitionSpec as P


def body(base_weights, factor_down, factor_up, presence, serving_order):
    up_whole = lax.all_gather(factor_up, "col", axis=1, tiled=True)
    down_whole = lax.all_gather(factor_down, "row", axis=2, tiled=True)
    delta = jnp.einsum(
        "edr,erf->edf",
        down_whole,
        up_whole,
        precision=lax.Precision.HIGHEST,
        preferred_element_type=jnp.float32,
    )
    flags = presence.reshape(-1).astype(jnp.float32)
    merged = (base_weights + flags[:, None, None] * delta).astype(jnp.bfloat16)
    ordered = jnp.take(merged, serving_order, axis=0)
    return lax.all_to_all(ordered, "row", split_axis=0, concat_axis=2, tiled=True)


def solution(mesh):
    return jax.shard_map(
        body,
        mesh=mesh,
        in_specs=(P(None, "col", "row"), P(None, "col", "row"), P(None, "col", "row"), P(), P()),
        out_specs=P("row", "col", None),
        check_vma=False,
    )
```

profile of v0, /device:TPU:1, one launch (start us, length us, event | category | flops | bytes accessed | tf_op | source)
XLA Modules:
  0.0 238.6 jit_solution(14384866859411044720)
XLA Ops:
  6.5 0.0 all-gather.3.cloned.1.call-start
  6.5 0.7 all-gather.3.cloned.1.call-update
  7.3 0.0 all-gather.5.cloned.1.call-start
  7.3 1.4 copy.7
  8.7 0.0 all-gather.5.cloned.1.call-update
  8.7 0.7 convert_element_type.13
  9.4 0.1 convert_element_type.14
  9.5 0.7 compare_select_fusion
  10.1 0.7 compare_and_fusion
  10.8 79.8 %all-gather.3.cloned.1.call-done = f32[32,112,128]{1,2,0:T(8,128)} async-done(((f32[32,112,8]{1,2,0:T(8,128)}), f32[32,112,128]{1,2,0:T(8,128)}) %all-gather.3.cloned.1.call-update) | async-done | bytes 1835024 | tf_op jit(solution)/shard_map/all_gather | solution.py:9
  90.6 102.4 %all-gather.5.cloned.1.call-done = f32[32,128,128]{2,0,1:T(8,128)} async-done(((f32[32,2,128]{2,0,1:T(8,128)}), f32[32,128,128]{2,0,1:T(8,128)}) %all-gather.5.cloned.1.call-update) | async-done | bytes 2097168 | tf_op jit(solution)/shard_map/all_gather | solution.py:8
  193.0 7.3 %add_convert_fusion = bf16[32,112,128]{2,1,0:T(8,128)(2,1)S(1)} fusion(f32[32,112,128]{2,1,0:T(8,128)} %param.5, f32[32,112,128]{1,2,0:T(8,128)} %all-gather.3.cloned.1.call-done, f32[32,128,128]{2,0,1:T(8,128)} %all-gather.5.cloned.1.call-done, f32[32]{0:T(128)S(1)} %convert_element_type.14), kind=kOutput, calls=%fused_computation.3 | convolution fusion | flops 706019328 | bytes 6684800 | tf_op jit(solution)/shard_map/edr,erf->edf/dot_general | solution.py:10
  200.3 0.7 gather_fusion
  201.1 0.2 broadcast_select_fusion
  201.2 29.3 %all_to_all.18 = bf16[32,112,128]{2,1,0:T(8,128)(2,1)S(1)} all-to-all(bf16[32,112,128]{2,1,0:T(8,128)(2,1)S(1)} %broadcast_select_fusion), channel_id=1, replica_groups=mesh['row'=16,'col'=64] {'row'}, dimensions={0} | all-to-all | bytes 1835008 | tf_op jit(solution)/shard_map/all_to_all | solution.py:20
  230.6 1.2 copy.16
  (1 shorter events, 0.0 us)
Async XLA Ops:
  6.5 84.1 %all-gather.3.cloned.1.call-start = ((), (), s32[]{:S(2)}) async-start(), calls=%async_computation.1 | async-start | bytes 2228224 | tf_op jit(solution)/shard_map/all_gather | solution.py:9
  7.3 185.7 %all-gather.5.cloned.1.call-start = ((), (), s32[]{:S(2)}) async-start(), calls=%async_computation.2 | async-start | bytes 2129920 | tf_op jit(solution)/shard_map/all_gather | solution.py:8
Sparse Core Ops, SparseCore 0:
  9.9 80.6 all-gather.2
  95.2 97.8 all-gather.4
where the time goes:
time: 241 us; the launch traced here: 239 us
  waiting for transfers between devices  183 us (76%)
  blocking collectives  29.3 us (12%)
  between operations  13.4 us (6%)
  matrix products  7.34 us (3%)
  local copies, waits for them, and re-layouts  3.36 us (1%)
    all_gather x1, waiting for transfers between devices, body(): up_whole = lax.all_gather(factor_up, 'col', axis=1, tiled=True)  102 us
    all_gather x1, waiting for transfers between devices, body(): down_whole = lax.all_gather(factor_down, 'row', axis=2, tiled=True)  79.8 us
    all_to_all x1, blocking collectives, body(): lax.all_to_all(ordered, 'row', split_axis=0, concat_axis=2, tiled=True)  29.3 us
    dot_general x1, matrix products, body(): jnp.einsum('edr,erf->edf', down_whole, up_whole, precision=lax.Precision....  7.34 us
  transfers between devices with their start and end apart: 2, of which 2 were waited for; matrix products, arithmetic and copies ran while one was open for 1% of the time, Pallas kernels for 0%

commit v1 on v0

v1 whole, which is shorter than its diff:
```python
import functools

import jax
import jax.numpy as jnp
from jax import lax
from jax.experimental import pallas as pl
from jax.experimental.pallas import tpu as pltpu
from jax.sharding import Mesh, PartitionSpec as P

TOP = 32767.0
BASE_MAX = 6.0
DOWN_MAX = 6.0
UP_MAX = 0.5
PAIRS = 16
ROWS = 112
TILE = 128
RANKS = 8
FF = 2048


def code_of(most, bound):
    root = jnp.sqrt(jnp.sqrt(most * (1.0 / bound)))
    return jnp.clip(jnp.ceil(root * TOP), 1.0, TOP)


def step_of(code, bound):
    part = code * (1.0 / TOP)
    part = part * part
    return part * part * (bound / TOP)


def coded(values, code, bound):
    return jnp.clip(jnp.round(values / step_of(code, bound)), -TOP, TOP)


def to16(values):
    return values.astype(jnp.int32).astype(jnp.int16)


def pack_kernel(per, order_ref, base_ref, down_ref, up_ref, out_ref, up_rows):
    first = pl.program_id(0) * per
    row8 = lax.broadcasted_iota(jnp.int32, (8, TILE), 0)
    lane = lax.broadcasted_iota(jnp.int32, (8, TILE), 1)
    up_rows[...] = jnp.zeros_like(up_rows)
    for p in range(per):
        downs, base_codes = [], []
        for e in range(2):
            expert = order_ref[(first + p) * 2 + e]
            tile = base_ref[expert]
            code = code_of(jnp.max(jnp.abs(tile), axis=0, keepdims=True), BASE_MAX)
            inverse = 1.0 / step_of(code, BASE_MAX)
            out_ref[p, e, 0:ROWS, :] = to16(jnp.clip(jnp.round(tile * inverse), -TOP, TOP))
            base_codes.append(code)
            factor = down_ref[expert]
            most = jnp.max(jnp.abs(factor), axis=1, keepdims=True)
            code = code_of(jnp.broadcast_to(most, (RANKS, TILE)), DOWN_MAX)
            wide = jnp.concatenate([factor, jnp.zeros((RANKS, TILE - ROWS), jnp.float32)], axis=1)
            downs.append(jnp.where(lane < ROWS, coded(wide, code, DOWN_MAX), code))
            up_rows[2 * e : 2 * e + 2, :] = up_ref[expert]
        low = (row8 & 2) == 0
        own = jnp.where(low, downs[0], pltpu.roll(downs[1], 2, 0))
        other = jnp.where(low, pltpu.roll(downs[0], 6, 0), downs[1])
        out_ref[p, 0, ROWS:TILE, :] = to16(jnp.concatenate([own, other], axis=0))
        ups = up_rows[...]
        most = jnp.max(jnp.abs(ups), axis=1, keepdims=True)
        code = code_of(jnp.broadcast_to(most, (8, TILE)), UP_MAX)
        head = jnp.where(row8 < 4, coded(ups, code, UP_MAX), pltpu.roll(code, 4, 0))
        tail = jnp.where(row8 == 0, base_codes[0], jnp.where(row8 == 1, base_codes[1], 0.0))
        out_ref[p, 1, ROWS:TILE, :] = to16(jnp.concatenate([head, tail], axis=0))


def pack(order, base, down, up):
    per = 4
    return pl.pallas_call(
        functools.partial(pack_kernel, per),
        grid_spec=pltpu.PrefetchScalarGridSpec(
            num_scalar_prefetch=1,
            grid=(PAIRS // per,),
            in_specs=[
                pl.BlockSpec(base.shape, lambda i, o: (0, 0, 0)),
                pl.BlockSpec(down.shape, lambda i, o: (0, 0, 0)),
                pl.BlockSpec(up.shape, lambda i, o: (0, 0, 0)),
            ],
            out_specs=pl.BlockSpec((per, 2, TILE, TILE), lambda i, o: (i, 0, 0, 0)),
            scratch_shapes=[pltpu.VMEM((8, TILE), jnp.float32)],
        ),
        out_shape=jax.ShapeDtypeStruct((PAIRS, 2, TILE, TILE), jnp.int16),
        compiler_params=pltpu.CompilerParams(vmem_limit_bytes=24 * 2**20),
        cost_estimate=pl.CostEstimate(flops=4_000_000, bytes_accessed=3_000_000, transcendentals=0),
    )(order, base, down, up)


def merge_kernel(per, order_ref, flag_ref, place_ref, tile_ref, down_ref, own_ref, other_ref, own_code, other_code, out_ref, left_hi, left_lo):
    row, core = place_ref[0], place_ref[1]

    @pl.when(pl.program_id(0) == 0)
    def _():
        flags = [flag_ref[order_ref[2 * row + e]].astype(jnp.float32) for e in range(2)]
        rows = down_ref[:, 0, :, :].astype(jnp.float32)
        halves = [rows[:, 0:8, :].reshape(TILE, TILE), rows[:, 8:16, :].reshape(TILE, TILE)]
        mine = jnp.where(core == 0, halves[0], halves[1])
        theirs = jnp.where(core == 0, halves[1], halves[0])
        expert = (lax.broadcasted_iota(jnp.int32, (TILE, TILE), 0) >> 1) & 1
        for h, (factor, code_ref) in enumerate(((mine, own_code), (theirs, other_code))):
            scale = step_of(factor[:, ROWS : ROWS + 1], DOWN_MAX) * step_of(code_ref[...].astype(jnp.float32), UP_MAX)
            factor = factor * scale
            for e in range(2):
                part = jnp.where(expert == e, factor * flags[e], 0.0).T[0:ROWS, :]
                high = part.astype(jnp.bfloat16)
                left_hi[e * ROWS : (e + 1) * ROWS, h * TILE : (h + 1) * TILE] = high
                left_lo[e * ROWS : (e + 1) * ROWS, h * TILE : (h + 1) * TILE] = (part - high.astype(jnp.float32)).astype(jnp.bfloat16)

    right = jnp.concatenate([own_ref[...], other_ref[...]], axis=0).astype(jnp.float32)
    high = right.astype(jnp.bfloat16)
    low = (right - high.astype(jnp.float32)).astype(jnp.bfloat16)
    dot = functools.partial(jnp.dot, preferred_element_type=jnp.float32)
    delta = dot(left_hi[...], high) + (dot(left_lo[...], high) + dot(left_hi[...], low))
    for s in range(per):
        codes = tile_ref[s, 1, ROWS:TILE, :].astype(jnp.float32)
        for e in range(2):
            base = tile_ref[s, e, 0:ROWS, :].astype(jnp.float32) * step_of(codes[8 + e : 9 + e, :], BASE_MAX)
            total = base + delta[e * ROWS : (e + 1) * ROWS, s * TILE : (s + 1) * TILE]
            out_ref[e, :, s * TILE : (s + 1) * TILE] = total.astype(jnp.bfloat16)


def merge(order, flags, place, tiles, own, other):
    per = 4
    wide = per * TILE
    last = FF // TILE
    half = pl.BlockSpec((TILE, wide), lambda i, *_: (0, i))
    code = pl.BlockSpec((TILE, TILE), lambda i, *_: (0, last))
    return pl.pallas_call(
        functools.partial(merge_kernel, per),
        grid_spec=pltpu.PrefetchScalarGridSpec(
            num_scalar_prefetch=3,
            grid=(PAIRS // per,),
            in_specs=[
                pl.BlockSpec((per, 2, TILE, TILE), lambda i, *_: (i, 0, 0, 0)),
                pl.BlockSpec((PAIRS, 1, 16, TILE), lambda i, *_: (0, 0, ROWS // 16, 0)),
                half,
                half,
                code,
                code,
            ],
            out_specs=pl.BlockSpec((2, ROWS, wide), lambda i, *_: (0, 0, i)),
            scratch_shapes=[pltpu.VMEM((2 * ROWS, 2 * TILE), jnp.bfloat16)] * 2,
        ),
        out_shape=jax.ShapeDtypeStruct((2, ROWS, FF), jnp.bfloat16),
        compiler_params=pltpu.CompilerParams(vmem_limit_bytes=24 * 2**20),
        cost_estimate=pl.CostEstimate(flops=700_000_000, bytes_accessed=4_000_000, transcendentals=0),
    )(order, flags, place, tiles, tiles, own, other, own, other)


def body(base_weights, factor_down, factor_up, presence, serving_order):
    place = jnp.stack([lax.axis_index("row"), lax.axis_index("core")]).astype(jnp.int32)
    sent = pack(serving_order, base_weights, jnp.swapaxes(factor_down, 1, 2), factor_up)
    tiles = lax.all_to_all(sent, "row", split_axis=0, concat_axis=0, tiled=True)

    rows = tiles[:, 1, ROWS : ROWS + 8, :].astype(jnp.float32)
    codes = rows[:, 4:8]
    most = jnp.max(codes, axis=0)
    ratio = codes / most
    ratio = ratio * ratio
    ups = jnp.clip(jnp.round(rows[:, 0:4] * (ratio * ratio)), -TOP, TOP)
    ups = jnp.concatenate([ups, most[None]], axis=0).astype(jnp.int16)
    ups = jnp.transpose(ups, (1, 0, 2)).reshape(4, FF + TILE)
    own = lax.all_to_all(jnp.broadcast_to(ups[None], (32,) + ups.shape), ("y", "xh"), split_axis=0, concat_axis=0, tiled=True)
    own = own.reshape(TILE, FF + TILE)
    other = lax.ppermute(own, "core", [(0, 1), (1, 0)])
    return merge(serving_order, presence.reshape(-1), place, tiles, own, other)


def solution(mesh):
    fine = Mesh(mesh.devices.reshape(16, 8, 4, 2), ("row", "y", "xh", "core"))
    col = ("y", "xh", "core")
    return jax.shard_map(
        body,
        mesh=fine,
        in_specs=(P(None, col, "row"), P(None, col, "row"), P(None, col, "row"), P(), P()),
        out_specs=P("row", col, None),
        check_vma=False,
    )
```

time: 241 us -> 89.3 us (0.37)
  the two profiles are of different devices: /device:TPU:1 before, /device:TPU:131 now
where the time goes in v1:
time: 89.3 us; the launch traced here: 88.9 us
  blocking collectives  75.1 us (84%)
  Pallas kernels  5.16 us (6%)
  local copies, waits for them, and re-layouts  4.2 us (5%)
  starting transfers between devices  2.87 us (3%)
  waiting for transfers between devices  1.39 us (2%)
    all_to_all x1, blocking collectives, body(): tiles = lax.all_to_all(sent, 'row', split_axis=0, concat_axis=0, tiled=True)  42.6 us
    all_to_all x1, blocking collectives, body(): lax.all_to_all(jnp.broadcast_to(ups[None], (32,) + ups.shape), ('y', 'xh'...  32.4 us
    unnamed x12, local copies, waits for them, and re-layouts  3.82 us
    pallas_call x1, Pallas kernels, merge(): pl.pallas_call(functools.partial(merge_kernel, per), grid_spec=pltpu.Pref...  3.68 us
    ppermute x1, starting transfers between devices, body(): other = lax.ppermute(own, 'core', [(0, 1), (1, 0)])  2.87 us
  transfers between devices with their start and end apart: 1, of which 1 were waited for; matrix products, arithmetic and copies ran while one was open for 0% of the time, Pallas kernels for 0%

profile of v1, /device:TPU:131, one launch (start us, length us, event | category | flops | bytes accessed | tf_op | source)
XLA Modules:
  0.0 88.9 jit_solution(6525700103686143378)
XLA Ops:
  0.0 0.0 copy-start
  0.0 1.5 %copy-done = f32[32,112,128]{2,1,0:T(8,128)S(1)} copy-done((f32[32,112,128]{2,1,0:T(8,128)S(1)}, f32[32,112,128]{2,1,0:T(8,128)}, u32[]{:S(2)}) %copy-start) | copy-done | bytes 1835032
  1.5 0.0 copy-start.1
  1.5 0.9 %copy-done.1 = f32[32,112,8]{1,2,0:T(8,128)S(1)} copy-done((f32[32,112,8]{1,2,0:T(8,128)S(1)}, f32[32,112,8]{1,2,0:T(8,128)}, u32[]{:S(2)}) %copy-start.1) | copy-done | bytes 114712
  2.4 0.0 copy-start.2
  2.4 0.8 copy-done.2
  3.2 0.0 copy-start.3
  3.2 0.7 copy-done.3
  3.8 1.5 %shard_map.55 = s16[16,2,128,128]{3,2,1,0:T(8,128)(2,1)S(1)} custom-call(s32[32]{0:T(128)S(1)} %copy-done.3, f32[32,112,128]{2,1,0:T(8,128)S(1)} %copy-done, f32[32,8,112]{2,1,0:T(8,128)S(1)} %bitcast.14, f32[32,2,128]{2,1,0:T(2,128)S(1)} %copy-done.2), custom_call_target="tpu_custom_call" | custom-call | flops 4000000 | bytes 3000000 | tf_op jit(solution)/shard_map/pallas_call | solution.py:74
  5.3 42.6 %all_to_all.10.tile_ref.down_ref = s16[16,2,128,128]{3,2,1,0:T(8,128)(2,1)S(1)} all-to-all(s16[16,2,128,128]{3,2,1,0:T(8,128)(2,1)S(1)} %shard_map.55), channel_id=1, replica_groups=mesh['row'=16,'y'=8,'xh'=4,'core'=2] {'row'}, dimensions={0} | all-to-all | bytes 2097152 | tf_op jit(solution)/shard_map/all_to_all | solution.py:157
  47.9 0.0 copy-start.5
  47.9 0.0 copy-start.4
  48.1 0.1 broadcast_in_dim.14
  48.2 32.4 %all_to_all.11 = s16[32,4,2176]{2,1,0:T(4,128)(2,1)S(1)} all-to-all(s16[32,4,2176]{2,1,0:T(4,128)(2,1)S(1)} %broadcast_in_dim.14), channel_id=1, replica_groups=mesh['row'=16,'y'=8,'xh'=4,'core'=2] {'y','xh'}, dimensions={0} | all-to-all | bytes 1114112 | tf_op jit(solution)/shard_map/all_to_all | solution.py:167
  80.6 0.2 reshape.11.own_ref.own_code
  80.8 2.9 %collective-permute-start = (s16[128,2176]{1,0:T(8,128)(2,1)S(1)}, s16[128,2176]{1,0:T(8,128)(2,1)S(1)}, u32[]{:S(2)}, u32[]{:S(2)}) collective-permute-start(s16[128,2176]{1,0:T(8,128)(2,1)S(1)} %reshape.11.own_ref.own_code), channel_id=1, source_target_pairs={{0,1},{1,0},{2,3},{3,2},{4,5},{5,4},{6,7},{7,6},{8,9},{9,8},{10,11... | collective-permute-start | bytes 1671176 | tf_op jit(solution)/shard_map/ppermute | solution.py:169
  83.7 0.0 copy-done.5
  83.7 0.1 reshape.10.flag_ref
  83.8 0.1 pad_add_fusion.place_ref
  83.8 1.4 %collective-permute-done.other_ref.other_code = s16[128,2176]{1,0:T(8,128)(2,1)S(1)} collective-permute-done((s16[128,2176]{1,0:T(8,128)(2,1)S(1)}, s16[128,2176]{1,0:T(8,128)(2,1)S(1)}, u32[]{:S(2)}, u32[]{:S(2)}) %collective-permute-start) | collective-permute-done | bytes 557088 | tf_op jit(solution)/shard_map/ppermute | solution.py:169
  85.2 0.0 copy-done.4
  85.2 3.7 %shard_map.56 = bf16[2,112,2048]{2,1,0:T(8,128)(2,1)} custom-call(s32[32]{0:T(128)S(1)} %copy-done.4, s32[32]{0:T(128)S(1)} %reshape.10.flag_ref, s32[2]{0:T(128)S(1)} %pad_add_fusion.place_ref, s16[16,2,128,128]{3,2,1,0:T(8,128)(2,1)S(1)} %all_to_all.10.tile_ref.down_ref, s16[16,2,128,128]{3,2,1,0:T(8,128)(2,1)S(1)} %all_to_all.10.tile_ref.down_ref, ...), custom_call_target="tpu_custom_call" | custom-call | flops 700000000 | bytes 4000000 | tf_op jit(solution)/shard_map/pallas_call | solution.py:132
  (5 shorter events, 0.1 us)
Async XLA Ops:
  0.0 1.5 %copy-start = (f32[32,112,128]{2,1,0:T(8,128)S(1)}, f32[32,112,128]{2,1,0:T(8,128)}, u32[]{:S(2)}) copy-start(f32[32,112,128]{2,1,0:T(8,128)} %base_ref.1) | copy-start | bytes 5505028
  1.5 0.9 %copy-start.1 = (f32[32,112,8]{1,2,0:T(8,128)S(1)}, f32[32,112,8]{1,2,0:T(8,128)}, u32[]{:S(2)}) copy-start(f32[32,112,8]{1,2,0:T(8,128)} %param.6) | copy-start | bytes 344068
  2.4 0.8 copy-start.2
  3.2 0.7 copy-start.3
  47.9 35.7 %copy-start.5 = (s32[2,16]{1,0:T(2,128)S(1)}, s32[2,16]{1,0:T(2,128)}, u32[]{:S(2)}) copy-start(s32[2,16]{1,0:T(2,128)} %param.8) | copy-start | bytes 388
  47.9 37.3 %copy-start.4 = (s32[32]{0:T(128)S(1)}, s32[32]{0:T(128)}, u32[]{:S(2)}) copy-start(s32[32]{0:T(128)} %order_ref.3) | copy-start | bytes 388
  80.8 4.4 %collective-permute-start = (s16[128,2176]{1,0:T(8,128)(2,1)S(1)}, s16[128,2176]{1,0:T(8,128)(2,1)S(1)}, u32[]{:S(2)}, u32[]{:S(2)}) collective-permute-start(s16[128,2176]{1,0:T(8,128)(2,1)S(1)} %reshape.11.own_ref.own_code), channel_id=1, source_target_pairs={{0,1},{1,0},{2,3},{3,2},{4,5},{5,4},{6,7},{7,6},{8,9},{9,8},{10,11... | collective-permute-start | bytes 1671176 | tf_op jit(solution)/shard_map/ppermute | solution.py:169

commit v2 on v1

--- a/solution.py
+++ b/solution.py
@@ -37,11 +37,50 @@
     return values.astype(jnp.int32).astype(jnp.int16)
 
 
-def pack_kernel(per, order_ref, base_ref, down_ref, up_ref, out_ref, up_rows):
+def spread_kernel(order_ref, up_ref, out_ref):
+    for p in range(PAIRS):
+        rows = jnp.concatenate([up_ref[order_ref[2 * p]], up_ref[order_ref[2 * p + 1]]] * 2, axis=0)
+        for y in range(0, 32, 8):
+            out_ref[p, y : y + 8, :] = rows
+
+
+def spread(order, up):
+    return pl.pallas_call(
+        spread_kernel,
+        in_specs=[pl.BlockSpec(memory_space=pltpu.SMEM), pl.BlockSpec(memory_space=pltpu.VMEM)],
+        out_specs=pl.BlockSpec(memory_space=pltpu.VMEM),
+        out_shape=jax.ShapeDtypeStruct((PAIRS, 32, TILE), jnp.float32),
+        compiler_params=pltpu.CompilerParams(vmem_limit_bytes=4 * 2**20),
+        cost_estimate=pl.CostEstimate(flops=0, bytes_accessed=300_000, transcendentals=0),
+    )(order, up)
+
+
+def code_kernel(up_ref, out_ref):
+    most = jnp.zeros((32, TILE), jnp.float32)
+    for r in range(PAIRS):
+        most = jnp.maximum(most, jnp.abs(up_ref[r]))
+    code = code_of(jnp.broadcast_to(jnp.max(most, axis=1, keepdims=True), (32, TILE)), UP_MAX)
+    inverse = 1.0 / step_of(code, UP_MAX)
+    for r in range(PAIRS):
+        out_ref[:, r * TILE : (r + 1) * TILE] = to16(jnp.clip(jnp.round(up_ref[r] * inverse), -TOP, TOP))
+    out_ref[:, FF : FF + TILE] = to16(code)
+
+
+def code_up(up):
+    return pl.pallas_call(
+        code_kernel,
+        in_specs=[pl.BlockSpec(memory_space=pltpu.VMEM)],
+        out_specs=pl.BlockSpec(memory_space=pltpu.VMEM),
+        out_shape=jax.ShapeDtypeStruct((32, FF + TILE), jnp.int16),
+        compiler_params=pltpu.CompilerParams(vmem_limit_bytes=4 * 2**20),
+        cost_estimate=pl.CostEstimate(flops=500_000, bytes_accessed=400_000, transcendentals=0),
+    )(up)
+
+
+def pack_kernel(per, order_ref, base_ref, down_ref, out_ref):
     first = pl.program_id(0) * per
     row8 = lax.broadcasted_iota(jnp.int32, (8, TILE), 0)
     lane = lax.broadcasted_iota(jnp.int32, (8, TILE), 1)
-    up_rows[...] = jnp.zeros_like(up_rows)
     for p in range(per):
         downs, base_codes = [], []
         for e in range(2):
@@ -56,20 +95,15 @@
             code = code_of(jnp.broadcast_to(most, (RANKS, TILE)), DOWN_MAX)
             wide = jnp.concatenate([factor, jnp.zeros((RANKS, TILE - ROWS), jnp.float32)], axis=1)
             downs.append(jnp.where(lane < ROWS, coded(wide, code, DOWN_MAX), code))
-            up_rows[2 * e : 2 * e + 2, :] = up_ref[expert]
         low = (row8 & 2) == 0
         own = jnp.where(low, downs[0], pltpu.roll(downs[1], 2, 0))
         other = jnp.where(low, pltpu.roll(downs[0], 6, 0), downs[1])
         out_ref[p, 0, ROWS:TILE, :] = to16(jnp.concatenate([own, other], axis=0))
-        ups = up_rows[...]
-        most = jnp.max(jnp.abs(ups), axis=1, keepdims=True)
-        code = code_of(jnp.broadcast_to(most, (8, TILE)), UP_MAX)
-        head = jnp.where(row8 < 4, coded(ups, code, UP_MAX), pltpu.roll(code, 4, 0))
-        tail = jnp.where(row8 == 0, base_codes[0], jnp.where(row8 == 1, base_codes[1], 0.0))
-        out_ref[p, 1, ROWS:TILE, :] = to16(jnp.concatenate([head, tail], axis=0))
-
-
-def pack(order, base, down, up):
+        head = jnp.where(row8 == 0, base_codes[0], jnp.where(row8 == 1, base_codes[1], 0.0))
+        out_ref[p, 1, ROWS:TILE, :] = to16(jnp.concatenate([head, jnp.zeros_like(head)], axis=0))
+
+
+def pack(order, base, down):
     per = 4
     return pl.pallas_call(
         functools.partial(pack_kernel, per),
@@ -79,19 +113,28 @@
             in_specs=[
                 pl.BlockSpec(base.shape, lambda i, o: (0, 0, 0)),
                 pl.BlockSpec(down.shape, lambda i, o: (0, 0, 0)),
-                pl.BlockSpec(up.shape, lambda i, o: (0, 0, 0)),
             ],
             out_specs=pl.BlockSpec((per, 2, TILE, TILE), lambda i, o: (i, 0, 0, 0)),
-            scratch_shapes=[pltpu.VMEM((8, TILE), jnp.float32)],
         ),
         out_shape=jax.ShapeDtypeStruct((PAIRS, 2, TILE, TILE), jnp.int16),
         compiler_params=pltpu.CompilerParams(vmem_limit_bytes=24 * 2**20),
         cost_estimate=pl.CostEstimate(flops=4_000_000, bytes_accessed=3_000_000, transcendentals=0),
-    )(order, base, down, up)
+    )(order, base, down)
+
+
+def sorted_rows(rows, xh):
+    i = lax.broadcasted_iota(jnp.int32, (TILE, TILE), 0)
+    j = lax.broadcasted_iota(jnp.int32, (TILE, TILE), 1)
+    source = (((i >> 2) & 7) << 4) | (((i >> 5) ^ xh) << 2) | (i & 3)
+    pick = jnp.where(j == source, 1.0, 0.0).astype(jnp.bfloat16)
+    high = rows.astype(jnp.bfloat16)
+    low = (rows - high.astype(jnp.float32)).astype(jnp.bfloat16)
+    dot = functools.partial(jnp.dot, preferred_element_type=jnp.float32)
+    return dot(pick, high) + dot(pick, low)
 
 
 def merge_kernel(per, order_ref, flag_ref, place_ref, tile_ref, down_ref, own_ref, other_ref, own_code, other_code, out_ref, left_hi, left_lo):
-    row, core = place_ref[0], place_ref[1]
+    row, xh, core = place_ref[0], place_ref[1], place_ref[2]
 
     @pl.when(pl.program_id(0) == 0)
     def _():
@@ -102,6 +145,7 @@
         theirs = jnp.where(core == 0, halves[1], halves[0])
         expert = (lax.broadcasted_iota(jnp.int32, (TILE, TILE), 0) >> 1) & 1
         for h, (factor, code_ref) in enumerate(((mine, own_code), (theirs, other_code))):
+            factor = sorted_rows(factor, xh)
             scale = step_of(factor[:, ROWS : ROWS + 1], DOWN_MAX) * step_of(code_ref[...].astype(jnp.float32), UP_MAX)
             factor = factor * scale
             for e in range(2):
@@ -118,7 +162,7 @@
     for s in range(per):
         codes = tile_ref[s, 1, ROWS:TILE, :].astype(jnp.float32)
         for e in range(2):
-            base = tile_ref[s, e, 0:ROWS, :].astype(jnp.float32) * step_of(codes[8 + e : 9 + e, :], BASE_MAX)
+            base = tile_ref[s, e, 0:ROWS, :].astype(jnp.float32) * step_of(codes[e : e + 1, :], BASE_MAX)
             total = base + delta[e * ROWS : (e + 1) * ROWS, s * TILE : (s + 1) * TILE]
             out_ref[e, :, s * TILE : (s + 1) * TILE] = total.astype(jnp.bfloat16)
 
@@ -152,20 +196,15 @@
 
 
 def body(base_weights, factor_down, factor_up, presence, serving_order):
-    place = jnp.stack([lax.axis_index("row"), lax.axis_index("core")]).astype(jnp.int32)
-    sent = pack(serving_order, base_weights, jnp.swapaxes(factor_down, 1, 2), factor_up)
+    place = jnp.stack([lax.axis_index("row"), lax.axis_index("xh"), lax.axis_index("core")]).astype(jnp.int32)
+    ups = spread(serving_order, factor_up).reshape(128, 4, TILE)
+    ups = lax.all_to_all(ups, ("row", "y"), split_axis=0, concat_axis=0, tiled=True)
+    sent = pack(serving_order, base_weights, jnp.swapaxes(factor_down, 1, 2))
     tiles = lax.all_to_all(sent, "row", split_axis=0, concat_axis=0, tiled=True)
 
-    rows = tiles[:, 1, ROWS : ROWS + 8, :].astype(jnp.float32)
-    codes = rows[:, 4:8]
-    most = jnp.max(codes, axis=0)
-    ratio = codes / most
-    ratio = ratio * ratio
-    ups = jnp.clip(jnp.round(rows[:, 0:4] * (ratio * ratio)), -TOP, TOP)
-    ups = jnp.concatenate([ups, most[None]], axis=0).astype(jnp.int16)
-    ups = jnp.transpose(ups, (1, 0, 2)).reshape(4, FF + TILE)
-    own = lax.all_to_all(jnp.broadcast_to(ups[None], (32,) + ups.shape), ("y", "xh"), split_axis=0, concat_axis=0, tiled=True)
-    own = own.reshape(TILE, FF + TILE)
+    own = code_up(ups.reshape(PAIRS, 32, TILE))
+    for apart in (1, 2):
+        own = jnp.concatenate([own, lax.ppermute(own, "xh", [(i, i ^ apart) for i in range(4)])], axis=0)
     other = lax.ppermute(own, "core", [(0, 1), (1, 0)])
     return merge(serving_order, presence.reshape(-1), place, tiles, own, other)
 

time: 89.3 us -> 91 us (1.019)
  the two profiles are of different devices: /device:TPU:131 before, /device:TPU:3 now
where the time goes in v2:
time: 91 us; the launch traced here: 90.5 us
  starting transfers between devices  39.4 us (43%)
  waiting for transfers between devices  38.5 us (42%)
  Pallas kernels  7.84 us (9%)
  local copies, waits for them, and re-layouts  4.55 us (5%)
    ppermute x2, waiting for transfers between devices, body(): lax.ppermute(own, 'xh', [(i, i ^ apart) for i in range(4)])  27.7 us
    all_to_all x1, starting transfers between devices, body(): lax.all_to_all(ups, ('row', 'y'), split_axis=0, concat_axis=0, tiled=True)  25 us
    all_to_all x1, waiting for transfers between devices, body(): lax.all_to_all(ups, ('row', 'y'), split_axis=0, concat_axis=0, tiled=True)  9.47 us
    ppermute x2, starting transfers between devices, body(): lax.ppermute(own, 'xh', [(i, i ^ apart) for i in range(4)])  8.46 us
    unnamed x14, local copies, waits for them, and re-layouts  4.47 us
    pallas_call x1, Pallas kernels, merge(): pl.pallas_call(functools.partial(merge_kernel, per), grid_spec=pltpu.Pref...  3.87 us
    all_to_all x1, starting transfers between devices, body(): tiles = lax.all_to_all(sent, 'row', split_axis=0, concat_axis=0, tiled=True)  3.55 us
    pallas_call x1, Pallas kernels, pack(): pl.pallas_call(functools.partial(pack_kernel, per), grid_spec=pltpu.Prefe...  2.54 us
  transfers between devices with their start and end apart: 5, of which 4 were waited for; matrix products, arithmetic and copies ran while one was open for 0% of the time, Pallas kernels for 3%

profile of v2, /device:TPU:3, one launch (start us, length us, event | category | flops | bytes accessed | tf_op | source)
XLA Modules:
  0.0 90.5 jit_solution(7831393517905575893)
XLA Ops:
  0.0 0.0 copy-start.2
  0.0 0.8 copy-done.2
  0.8 0.0 copy-start.3
  0.8 0.7 copy-done.3
  1.4 1.3 %shard_map.56 = f32[16,32,128]{2,1,0:T(8,128)} custom-call(s32[32]{0:T(128)S(1)} %copy-done.3, f32[32,2,128]{2,1,0:T(2,128)S(1)} %copy-done.2), custom_call_target="tpu_custom_call" | custom-call | bytes 300000 | tf_op jit(solution)/shard_map/pallas_call | solution.py:48
  2.7 25.0 %all-to-all-start.1 = ((f32[128,4,128]{2,1,0:T(4,128)}), f32[128,4,128]{2,1,0:T(4,128)S(1)}, u32[]{:S(2)}, u32[]{:S(2)}) async-start(f32[128,4,128]{2,1,0:T(4,128)} %bitcast.4), calls=%async_computation.1 | async-start | bytes 524288 | tf_op jit(solution)/shard_map/all_to_all | solution.py:201
  27.7 0.0 copy-start
  27.7 1.5 %copy-done = f32[32,112,128]{2,1,0:T(8,128)S(1)} copy-done((f32[32,112,128]{2,1,0:T(8,128)S(1)}, f32[32,112,128]{2,1,0:T(8,128)}, u32[]{:S(2)}) %copy-start) | copy-done | bytes 1835032
  29.2 0.0 copy-start.1
  29.2 0.9 copy-done.1
  30.1 0.0 copy-start.4
  30.1 0.7 copy-done.4
  30.7 2.5 %shard_map.55 = s16[16,2,128,128]{3,2,1,0:T(8,128)(2,1)} custom-call(s32[32]{0:T(128)S(1)} %copy-done.4, f32[32,112,128]{2,1,0:T(8,128)S(1)} %copy-done, f32[32,8,112]{2,1,0:T(8,128)S(1)} %bitcast.7), custom_call_target="tpu_custom_call" | custom-call | flops 4000000 | bytes 3000000 | tf_op jit(solution)/shard_map/pallas_call | solution.py:108
  33.3 0.0 copy-start.6
  33.3 0.0 copy-start.5
  33.3 9.5 %all-to-all-done.1 = f32[128,4,128]{2,1,0:T(4,128)S(1)} async-done(((f32[128,4,128]{2,1,0:T(4,128)}), f32[128,4,128]{2,1,0:T(4,128)S(1)}, u32[]{:S(2)}, u32[]{:S(2)}) %all-to-all-start.1) | async-done | bytes 262176 | tf_op jit(solution)/shard_map/all_to_all | solution.py:201
  42.7 3.6 %all-to-all-start = ((s16[16,2,128,128]{3,2,1,0:T(8,128)(2,1)}), s16[16,2,128,128]{3,2,1,0:T(8,128)(2,1)S(1)}, u32[]{:S(2)}, u32[]{:S(2)}) async-start(s16[16,2,128,128]{3,2,1,0:T(8,128)(2,1)} %shard_map.55), calls=%async_computation | async-start | bytes 2097152 | tf_op jit(solution)/shard_map/all_to_all | solution.py:203
  46.3 0.2 shard_map.57
  46.5 4.0 %collective-permute-start = (s16[32,2176]{1,0:T(8,128)(2,1)S(1)}, s16[32,2176]{1,0:T(8,128)(2,1)S(1)}, u32[]{:S(2)}, u32[]{:S(2)}) collective-permute-start(s16[32,2176]{1,0:T(8,128)(2,1)S(1)} %shard_map.57), channel_id=1, source_target_pairs={{0,2},{2,0},{4,6},{6,4},{1,3},{3,1},{5,7},{7,5},{8,10},{10,8},{12,... | collective-permute-start | bytes 417800 | tf_op jit(solution)/shard_map/ppermute | solution.py:207
  50.5 12.8 %collective-permute-done = s16[32,2176]{1,0:T(8,128)(2,1)S(1)} collective-permute-done((s16[32,2176]{1,0:T(8,128)(2,1)S(1)}, s16[32,2176]{1,0:T(8,128)(2,1)S(1)}, u32[]{:S(2)}, u32[]{:S(2)}) %collective-permute-start) | collective-permute-done | bytes 139296 | tf_op jit(solution)/shard_map/ppermute | solution.py:207
  63.3 4.4 %collective-permute-start.1 = (s16[64,2176]{1,0:T(8,128)(2,1)S(1)}, s16[64,2176]{1,0:T(8,128)(2,1)S(1)}, u32[]{:S(2)}, u32[]{:S(2)}) collective-permute-start(s16[64,2176]{1,0:T(8,128)(2,1)S(1)} %pad_add_fusion.1), channel_id=1, source_target_pairs={{0,4},{2,6},{4,0},{6,2},{1,5},{3,7},{5,1},{7,3},{8,12},{10,14},{12... | collective-permute-start | bytes 835592 | tf_op jit(solution)/shard_map/ppermute | solution.py:207
  67.7 14.9 %collective-permute-done.1 = s16[64,2176]{1,0:T(8,128)(2,1)S(1)} collective-permute-done((s16[64,2176]{1,0:T(8,128)(2,1)S(1)}, s16[64,2176]{1,0:T(8,128)(2,1)S(1)}, u32[]{:S(2)}, u32[]{:S(2)}) %collective-permute-start.1) | collective-permute-done | bytes 278560 | tf_op jit(solution)/shard_map/ppermute | solution.py:207
  82.7 2.4 %collective-permute-start.2 = (s16[128,2176]{1,0:T(8,128)(2,1)S(1)}, s16[128,2176]{1,0:T(8,128)(2,1)S(1)}, u32[]{:S(2)}, u32[]{:S(2)}) collective-permute-start(s16[128,2176]{1,0:T(8,128)(2,1)S(1)} %pad_add_fusion.own_ref.own_code), channel_id=1, source_target_pairs={{0,1},{1,0},{2,3},{3,2},{4,5},{5,4},{6,7},{7,6},{8,9},{9,8},{10,11... | collective-permute-start | bytes 1671176 | tf_op jit(solution)/shard_map/ppermute | solution.py:208
  85.1 0.0 copy-done.6
  85.1 0.1 reshape.9.flag_ref
  85.2 0.1 pad_add_fusion.2.place_ref
  85.3 1.4 %collective-permute-done.2.other_ref.other_code = s16[128,2176]{1,0:T(8,128)(2,1)S(1)} collective-permute-done((s16[128,2176]{1,0:T(8,128)(2,1)S(1)}, s16[128,2176]{1,0:T(8,128)(2,1)S(1)}, u32[]{:S(2)}, u32[]{:S(2)}) %collective-permute-start.2) | collective-permute-done | bytes 557088 | tf_op jit(solution)/shard_map/ppermute | solution.py:208
  86.7 0.0 all-to-all-done.tile_ref.down_ref
  86.7 0.0 copy-done.5
  86.7 3.9 %shard_map.58 = bf16[2,112,2048]{2,1,0:T(8,128)(2,1)} custom-call(s32[32]{0:T(128)S(1)} %copy-done.5, s32[32]{0:T(128)S(1)} %reshape.9.flag_ref, s32[3]{0:T(128)S(1)} %pad_add_fusion.2.place_ref, s16[16,2,128,128]{3,2,1,0:T(8,128)(2,1)S(1)} %all-to-all-done.tile_ref.down_ref, s16[16,2,128,128]{3,2,1,0:T(8,128)(2,1)S(1)} %all-to-all-done.tile_ref.down_ref, ...), custom_call_target="tpu_custom_call" | custom-call | flops 700000000 | bytes 4000000 | tf_op jit(solution)/shard_map/pallas_call | solution.py:176
  (2 shorter events, 0.1 us)
Async XLA Ops:
  0.0 0.8 copy-start.2
  0.8 0.7 copy-start.3
  2.7 40.0 %all-to-all-start.1 = ((f32[128,4,128]{2,1,0:T(4,128)}), f32[128,4,128]{2,1,0:T(4,128)S(1)}, u32[]{:S(2)}, u32[]{:S(2)}) async-start(f32[128,4,128]{2,1,0:T(4,128)} %bitcast.4), calls=%async_computation.1 | async-start | bytes 524288 | tf_op jit(solution)/shard_map/all_to_all | solution.py:201
  27.7 1.5 %copy-start = (f32[32,112,128]{2,1,0:T(8,128)S(1)}, f32[32,112,128]{2,1,0:T(8,128)}, u32[]{:S(2)}) copy-start(f32[32,112,128]{2,1,0:T(8,128)} %base_ref.1) | copy-start | bytes 5505028
  29.2 0.9 copy-start.1
  30.1 0.7 copy-start.4
  33.3 51.9 %copy-start.6 = (s32[2,16]{1,0:T(2,128)S(1)}, s32[2,16]{1,0:T(2,128)}, u32[]{:S(2)}) copy-start(s32[2,16]{1,0:T(2,128)} %param.8) | copy-start | bytes 388
  33.3 53.4 %copy-start.5 = (s32[32]{0:T(128)S(1)}, s32[32]{0:T(128)}, u32[]{:S(2)}) copy-start(s32[32]{0:T(128)} %order_ref.5) | copy-start | bytes 388
  42.7 43.9 %all-to-all-start = ((s16[16,2,128,128]{3,2,1,0:T(8,128)(2,1)}), s16[16,2,128,128]{3,2,1,0:T(8,128)(2,1)S(1)}, u32[]{:S(2)}, u32[]{:S(2)}) async-start(s16[16,2,128,128]{3,2,1,0:T(8,128)(2,1)} %shard_map.55), calls=%async_computation | async-start | bytes 2097152 | tf_op jit(solution)/shard_map/all_to_all | solution.py:203
  46.5 16.8 %collective-permute-start = (s16[32,2176]{1,0:T(8,128)(2,1)S(1)}, s16[32,2176]{1,0:T(8,128)(2,1)S(1)}, u32[]{:S(2)}, u32[]{:S(2)}) collective-permute-start(s16[32,2176]{1,0:T(8,128)(2,1)S(1)} %shard_map.57), channel_id=1, source_target_pairs={{0,2},{2,0},{4,6},{6,4},{1,3},{3,1},{5,7},{7,5},{8,10},{10,8},{12,... | collective-permute-start | bytes 417800 | tf_op jit(solution)/shard_map/ppermute | solution.py:207
  63.3 19.3 %collective-permute-start.1 = (s16[64,2176]{1,0:T(8,128)(2,1)S(1)}, s16[64,2176]{1,0:T(8,128)(2,1)S(1)}, u32[]{:S(2)}, u32[]{:S(2)}) collective-permute-start(s16[64,2176]{1,0:T(8,128)(2,1)S(1)} %pad_add_fusion.1), channel_id=1, source_target_pairs={{0,4},{2,6},{4,0},{6,2},{1,5},{3,7},{5,1},{7,3},{8,12},{10,14},{12... | collective-permute-start | bytes 835592 | tf_op jit(solution)/shard_map/ppermute | solution.py:207
  82.7 4.0 %collective-permute-start.2 = (s16[128,2176]{1,0:T(8,128)(2,1)S(1)}, s16[128,2176]{1,0:T(8,128)(2,1)S(1)}, u32[]{:S(2)}, u32[]{:S(2)}) collective-permute-start(s16[128,2176]{1,0:T(8,128)(2,1)S(1)} %pad_add_fusion.own_ref.own_code), channel_id=1, source_target_pairs={{0,1},{1,0},{2,3},{3,2},{4,5},{5,4},{6,7},{7,6},{8,9},{9,8},{10,11... | collective-permute-start | bytes 1671176 | tf_op jit(solution)/shard_map/ppermute | solution.py:208

commit v3 on v2

--- a/solution.py
+++ b/solution.py
@@ -40,8 +40,9 @@
 def spread_kernel(order_ref, up_ref, out_ref):
     for p in range(PAIRS):
         rows = jnp.concatenate([up_ref[order_ref[2 * p]], up_ref[order_ref[2 * p + 1]]] * 2, axis=0)
-        for y in range(0, 32, 8):
-            out_ref[p, y : y + 8, :] = rows
+        root = jnp.minimum(jnp.round(jnp.sqrt(jnp.sqrt(jnp.abs(rows) * (1.0 / UP_MAX))) * TOP), TOP)
+        root = jnp.where(rows < 0.0, -root, root)
+        out_ref[p] = to16(jnp.concatenate([root] * 4, axis=0))
 
 
 def spread(order, up):
@@ -49,7 +50,7 @@
         spread_kernel,
         in_specs=[pl.BlockSpec(memory_space=pltpu.SMEM), pl.BlockSpec(memory_space=pltpu.VMEM)],
         out_specs=pl.BlockSpec(memory_space=pltpu.VMEM),
-        out_shape=jax.ShapeDtypeStruct((PAIRS, 32, TILE), jnp.float32),
+        out_shape=jax.ShapeDtypeStruct((PAIRS, 32, TILE), jnp.int16),
         compiler_params=pltpu.CompilerParams(vmem_limit_bytes=4 * 2**20),
         cost_estimate=pl.CostEstimate(flops=0, bytes_accessed=300_000, transcendentals=0),
     )(order, up)
@@ -58,11 +59,13 @@
 def code_kernel(up_ref, out_ref):
     most = jnp.zeros((32, TILE), jnp.float32)
     for r in range(PAIRS):
-        most = jnp.maximum(most, jnp.abs(up_ref[r]))
-    code = code_of(jnp.broadcast_to(jnp.max(most, axis=1, keepdims=True), (32, TILE)), UP_MAX)
-    inverse = 1.0 / step_of(code, UP_MAX)
+        most = jnp.maximum(most, jnp.abs(up_ref[r].astype(jnp.float32)))
+    code = jnp.maximum(jnp.broadcast_to(jnp.max(most, axis=1, keepdims=True), (32, TILE)), 1.0)
+    inverse = 1.0 / code
     for r in range(PAIRS):
-        out_ref[:, r * TILE : (r + 1) * TILE] = to16(jnp.clip(jnp.round(up_ref[r] * inverse), -TOP, TOP))
+        part = up_ref[r].astype(jnp.float32) * inverse
+        part = part * part * part * jnp.abs(part)
+        out_ref[:, r * TILE : (r + 1) * TILE] = to16(jnp.clip(jnp.round(part * TOP), -TOP, TOP))
     out_ref[:, FF : FF + TILE] = to16(code)
 
 
@@ -122,10 +125,10 @@
     )(order, base, down)
 
 
-def sorted_rows(rows, xh):
+def sorted_rows(rows, yb):
     i = lax.broadcasted_iota(jnp.int32, (TILE, TILE), 0)
     j = lax.broadcasted_iota(jnp.int32, (TILE, TILE), 1)
-    source = (((i >> 2) & 7) << 4) | (((i >> 5) ^ xh) << 2) | (i & 3)
+    source = (((i >> 4) & 1) << 6) | (((i >> 5) ^ yb) << 4) | (i & 15)
     pick = jnp.where(j == source, 1.0, 0.0).astype(jnp.bfloat16)
     high = rows.astype(jnp.bfloat16)
     low = (rows - high.astype(jnp.float32)).astype(jnp.bfloat16)
@@ -134,7 +137,7 @@
 
 
 def merge_kernel(per, order_ref, flag_ref, place_ref, tile_ref, down_ref, own_ref, other_ref, own_code, other_code, out_ref, left_hi, left_lo):
-    row, xh, core = place_ref[0], place_ref[1], place_ref[2]
+    row, yb, core = place_ref[0], place_ref[1], place_ref[2]
 
     @pl.when(pl.program_id(0) == 0)
     def _():
@@ -145,7 +148,7 @@
         theirs = jnp.where(core == 0, halves[1], halves[0])
         expert = (lax.broadcasted_iota(jnp.int32, (TILE, TILE), 0) >> 1) & 1
         for h, (factor, code_ref) in enumerate(((mine, own_code), (theirs, other_code))):
-            factor = sorted_rows(factor, xh)
+            factor = sorted_rows(factor, yb)
             scale = step_of(factor[:, ROWS : ROWS + 1], DOWN_MAX) * step_of(code_ref[...].astype(jnp.float32), UP_MAX)
             factor = factor * scale
             for e in range(2):
@@ -196,22 +199,21 @@
 
 
 def body(base_weights, factor_down, factor_up, presence, serving_order):
-    place = jnp.stack([lax.axis_index("row"), lax.axis_index("xh"), lax.axis_index("core")]).astype(jnp.int32)
+    place = jnp.stack([lax.axis_index("row"), lax.axis_index("yb"), lax.axis_index("core")]).astype(jnp.int32)
     ups = spread(serving_order, factor_up).reshape(128, 4, TILE)
-    ups = lax.all_to_all(ups, ("row", "y"), split_axis=0, concat_axis=0, tiled=True)
+    ups = lax.all_to_all(ups, ("row", "ya", "xh"), split_axis=0, concat_axis=0, tiled=True)
     sent = pack(serving_order, base_weights, jnp.swapaxes(factor_down, 1, 2))
     tiles = lax.all_to_all(sent, "row", split_axis=0, concat_axis=0, tiled=True)
 
     own = code_up(ups.reshape(PAIRS, 32, TILE))
-    for apart in (1, 2):
-        own = jnp.concatenate([own, lax.ppermute(own, "xh", [(i, i ^ apart) for i in range(4)])], axis=0)
+    own = jnp.concatenate([own] + [lax.ppermute(own, "yb", [(i, i ^ apart) for i in range(4)]) for apart in (1, 2, 3)], axis=0)
     other = lax.ppermute(own, "core", [(0, 1), (1, 0)])
     return merge(serving_order, presence.reshape(-1), place, tiles, own, other)
 
 
 def solution(mesh):
-    fine = Mesh(mesh.devices.reshape(16, 8, 4, 2), ("row", "y", "xh", "core"))
-    col = ("y", "xh", "core")
+    fine = Mesh(mesh.devices.reshape(16, 2, 4, 4, 2), ("row", "ya", "yb", "xh", "core"))
+    col = ("ya", "yb", "xh", "core")
     return jax.shard_map(
         body,
         mesh=fine,

time: 91 us -> 81.8 us (0.90)
  the two profiles are of different devices: /device:TPU:3 before, /device:TPU:1 now
where the time goes in v3:
time: 81.8 us; the launch traced here: 81.3 us
  starting transfers between devices  47 us (57%)
  waiting for transfers between devices  21.6 us (26%)
  Pallas kernels  7.9 us (10%)
  local copies, waits for them, and re-layouts  4.55 us (6%)
    all_to_all x1, starting transfers between devices, body(): lax.all_to_all(ups, ('row', 'ya', 'xh'), split_axis=0, concat_axis=0, til...  30.1 us
    all_to_all x1, waiting for transfers between devices, body(): lax.all_to_all(ups, ('row', 'ya', 'xh'), split_axis=0, concat_axis=0, til...  9.78 us
    ppermute x3, starting transfers between devices, body(): lax.ppermute(own, 'yb', [(i, i ^ apart) for i in range(4)])  9.27 us
    ppermute x3, waiting for transfers between devices, body(): lax.ppermute(own, 'yb', [(i, i ^ apart) for i in range(4)])  6.47 us
    unnamed x14, local copies, waits for them, and re-layouts  4.47 us
    ppermute x1, starting transfers between devices, body(): other = lax.ppermute(own, 'core', [(0, 1), (1, 0)])  4.01 us
    all_to_all x1, waiting for transfers between devices, body(): tiles = lax.all_to_all(sent, 'row', split_axis=0, concat_axis=0, tiled=True)  3.93 us
    pallas_call x1, Pallas kernels, merge(): pl.pallas_call(functools.partial(merge_kernel, per), grid_spec=pltpu.Pref...  3.87 us
  transfers between devices with their start and end apart: 6, of which 4 were waited for; matrix products, arithmetic and copies ran while one was open for 0% of the time, Pallas kernels for 3%

profile of v3, /device:TPU:1, one launch (start us, length us, event | category | flops | bytes accessed | tf_op | source)
XLA Modules:
  0.0 81.3 jit_solution(13844358064975857908)
XLA Ops:
  0.0 0.0 copy-start.2
  0.0 0.8 copy-done.2
  0.8 0.0 copy-start.3
  0.8 0.7 copy-done.3
  1.4 1.3 %shard_map.56 = s16[16,32,128]{2,1,0:T(8,128)(2,1)} custom-call(s32[32]{0:T(128)S(1)} %copy-done.3, f32[32,2,128]{2,1,0:T(2,128)S(1)} %copy-done.2), custom_call_target="tpu_custom_call" | custom-call | bytes 300000 | tf_op jit(solution)/shard_map/pallas_call | solution.py:49
  2.7 30.1 %all-to-all-start.1 = ((s16[128,4,128]{2,1,0:T(4,128)(2,1)}), s16[128,4,128]{2,1,0:T(4,128)(2,1)S(1)}, u32[]{:S(2)}, u32[]{:S(2)}) async-start(s16[128,4,128]{2,1,0:T(4,128)(2,1)} %bitcast.4), calls=%async_computation.1 | async-start | bytes 262144 | tf_op jit(solution)/shard_map/all_to_all | solution.py:204
  32.8 0.0 copy-start
  32.8 1.5 %copy-done = f32[32,112,128]{2,1,0:T(8,128)S(1)} copy-done((f32[32,112,128]{2,1,0:T(8,128)S(1)}, f32[32,112,128]{2,1,0:T(8,128)}, u32[]{:S(2)}) %copy-start) | copy-done | bytes 1835032
  34.3 0.0 copy-start.1
  34.3 0.9 %copy-done.1 = f32[32,112,8]{1,2,0:T(8,128)S(1)} copy-done((f32[32,112,8]{1,2,0:T(8,128)S(1)}, f32[32,112,8]{1,2,0:T(8,128)}, u32[]{:S(2)}) %copy-start.1) | copy-done | bytes 114712
  35.2 0.0 copy-start.4
  35.2 0.7 copy-done.4
  35.9 2.6 %shard_map.55 = s16[16,2,128,128]{3,2,1,0:T(8,128)(2,1)} custom-call(s32[32]{0:T(128)S(1)} %copy-done.4, f32[32,112,128]{2,1,0:T(8,128)S(1)} %copy-done, f32[32,8,112]{2,1,0:T(8,128)S(1)} %bitcast.7), custom_call_target="tpu_custom_call" | custom-call | flops 4000000 | bytes 3000000 | tf_op jit(solution)/shard_map/pallas_call | solution.py:111
  38.4 0.0 copy-start.6
  38.4 0.0 copy-start.5
  38.4 9.8 %all-to-all-done.1 = s16[128,4,128]{2,1,0:T(4,128)(2,1)S(1)} async-done(((s16[128,4,128]{2,1,0:T(4,128)(2,1)}), s16[128,4,128]{2,1,0:T(4,128)(2,1)S(1)}, u32[]{:S(2)}, u32[]{:S(2)}) %all-to-all-start.1) | async-done | bytes 131104 | tf_op jit(solution)/shard_map/all_to_all | solution.py:204
  48.2 3.7 %all-to-all-start = ((s16[16,2,128,128]{3,2,1,0:T(8,128)(2,1)}), s16[16,2,128,128]{3,2,1,0:T(8,128)(2,1)S(1)}, u32[]{:S(2)}, u32[]{:S(2)}) async-start(s16[16,2,128,128]{3,2,1,0:T(8,128)(2,1)} %shard_map.55), calls=%async_computation | async-start | bytes 2097152 | tf_op jit(solution)/shard_map/all_to_all | solution.py:206
  51.9 0.2 shard_map.57
  52.1 2.9 %collective-permute-start.2 = (s16[32,2176]{1,0:T(8,128)(2,1)S(1)}, s16[32,2176]{1,0:T(8,128)(2,1)S(1)}, u32[]{:S(2)}, u32[]{:S(2)}) collective-permute-start(s16[32,2176]{1,0:T(8,128)(2,1)S(1)} %shard_map.57), channel_id=1, source_target_pairs={{0,24},{8,16},{16,8},{24,0},{1,25},{9,17},{17,9},{25,1},{2,26},{10... | collective-permute-start | bytes 417800 | tf_op jit(solution)/shard_map/ppermute | solution.py:209
  54.9 2.6 %collective-permute-start.1 = (s16[32,2176]{1,0:T(8,128)(2,1)S(1)}, s16[32,2176]{1,0:T(8,128)(2,1)S(1)}, u32[]{:S(2)}, u32[]{:S(2)}) collective-permute-start(s16[32,2176]{1,0:T(8,128)(2,1)S(1)} %shard_map.57), channel_id=1, source_target_pairs={{0,16},{8,24},{16,0},{24,8},{1,17},{9,25},{17,1},{25,9},{2,18},{10... | collective-permute-start | bytes 417800 | tf_op jit(solution)/shard_map/ppermute | solution.py:209
  57.6 3.8 %collective-permute-start = (s16[32,2176]{1,0:T(8,128)(2,1)S(1)}, s16[32,2176]{1,0:T(8,128)(2,1)S(1)}, u32[]{:S(2)}, u32[]{:S(2)}) collective-permute-start(s16[32,2176]{1,0:T(8,128)(2,1)S(1)} %shard_map.57), channel_id=1, source_target_pairs={{0,8},{8,0},{16,24},{24,16},{1,9},{9,1},{17,25},{25,17},{2,10},{10... | collective-permute-start | bytes 417800 | tf_op jit(solution)/shard_map/ppermute | solution.py:209
  61.4 0.0 collective-permute-done.2
  61.4 6.5 %collective-permute-done.1 = s16[32,2176]{1,0:T(8,128)(2,1)S(1)} collective-permute-done((s16[32,2176]{1,0:T(8,128)(2,1)S(1)}, s16[32,2176]{1,0:T(8,128)(2,1)S(1)}, u32[]{:S(2)}, u32[]{:S(2)}) %collective-permute-start.1) | collective-permute-done | bytes 139296 | tf_op jit(solution)/shard_map/ppermute | solution.py:209
  67.8 0.0 collective-permute-done
  67.9 4.0 %collective-permute-start.3 = (s16[128,2176]{1,0:T(8,128)(2,1)S(1)}, s16[128,2176]{1,0:T(8,128)(2,1)S(1)}, u32[]{:S(2)}, u32[]{:S(2)}) collective-permute-start(s16[128,2176]{1,0:T(8,128)(2,1)S(1)} %pad_add_fusion.own_ref.own_code), channel_id=1, source_target_pairs={{0,1},{1,0},{2,3},{3,2},{4,5},{5,4},{6,7},{7,6},{8,9},{9,8},{10,11... | collective-permute-start | bytes 1671176 | tf_op jit(solution)/shard_map/ppermute | solution.py:210
  71.9 0.0 copy-done.6
  71.9 0.1 reshape.9.flag_ref
  72.0 0.1 pad_add_fusion.1.place_ref
  72.1 1.4 %collective-permute-done.3.other_ref.other_code = s16[128,2176]{1,0:T(8,128)(2,1)S(1)} collective-permute-done((s16[128,2176]{1,0:T(8,128)(2,1)S(1)}, s16[128,2176]{1,0:T(8,128)(2,1)S(1)}, u32[]{:S(2)}, u32[]{:S(2)}) %collective-permute-start.3) | collective-permute-done | bytes 557088 | tf_op jit(solution)/shard_map/ppermute | solution.py:210
  73.5 3.9 %all-to-all-done.tile_ref.down_ref = s16[16,2,128,128]{3,2,1,0:T(8,128)(2,1)S(1)} async-done(((s16[16,2,128,128]{3,2,1,0:T(8,128)(2,1)}), s16[16,2,128,128]{3,2,1,0:T(8,128)(2,1)S(1)}, u32[]{:S(2)}, u32[]{:S(2)}) %all-to-all-start) | async-done | bytes 1048608 | tf_op jit(solution)/shard_map/all_to_all | solution.py:206
  77.4 0.0 copy-done.5
  77.4 3.9 %shard_map.58 = bf16[2,112,2048]{2,1,0:T(8,128)(2,1)} custom-call(s32[32]{0:T(128)S(1)} %copy-done.5, s32[32]{0:T(128)S(1)} %reshape.9.flag_ref, s32[3]{0:T(128)S(1)} %pad_add_fusion.1.place_ref, s16[16,2,128,128]{3,2,1,0:T(8,128)(2,1)S(1)} %all-to-all-done.tile_ref.down_ref, s16[16,2,128,128]{3,2,1,0:T(8,128)(2,1)S(1)} %all-to-all-done.tile_ref.down_ref, ...), custom_call_target="tpu_custom_call" | custom-call | flops 700000000 | bytes 4000000 | tf_op jit(solution)/shard_map/pallas_call | solution.py:179
  (1 shorter events, 0.0 us)
Async XLA Ops:
  0.0 0.8 copy-start.2
  0.8 0.7 copy-start.3
  2.7 45.5 %all-to-all-start.1 = ((s16[128,4,128]{2,1,0:T(4,128)(2,1)}), s16[128,4,128]{2,1,0:T(4,128)(2,1)S(1)}, u32[]{:S(2)}, u32[]{:S(2)}) async-start(s16[128,4,128]{2,1,0:T(4,128)(2,1)} %bitcast.4), calls=%async_computation.1 | async-start | bytes 262144 | tf_op jit(solution)/shard_map/all_to_all | solution.py:204
  32.8 1.5 %copy-start = (f32[32,112,128]{2,1,0:T(8,128)S(1)}, f32[32,112,128]{2,1,0:T(8,128)}, u32[]{:S(2)}) copy-start(f32[32,112,128]{2,1,0:T(8,128)} %base_ref.1) | copy-start | bytes 5505028
  34.3 0.9 %copy-start.1 = (f32[32,112,8]{1,2,0:T(8,128)S(1)}, f32[32,112,8]{1,2,0:T(8,128)}, u32[]{:S(2)}) copy-start(f32[32,112,8]{1,2,0:T(8,128)} %param.6) | copy-start | bytes 344068
  35.2 0.7 copy-start.4
  38.4 33.5 %copy-start.6 = (s32[2,16]{1,0:T(2,128)S(1)}, s32[2,16]{1,0:T(2,128)}, u32[]{:S(2)}) copy-start(s32[2,16]{1,0:T(2,128)} %param.8) | copy-start | bytes 388
  38.4 39.0 %copy-start.5 = (s32[32]{0:T(128)S(1)}, s32[32]{0:T(128)}, u32[]{:S(2)}) copy-start(s32[32]{0:T(128)} %order_ref.5) | copy-start | bytes 388
  48.2 29.2 %all-to-all-start = ((s16[16,2,128,128]{3,2,1,0:T(8,128)(2,1)}), s16[16,2,128,128]{3,2,1,0:T(8,128)(2,1)S(1)}, u32[]{:S(2)}, u32[]{:S(2)}) async-start(s16[16,2,128,128]{3,2,1,0:T(8,128)(2,1)} %shard_map.55), calls=%async_computation | async-start | bytes 2097152 | tf_op jit(solution)/shard_map/all_to_all | solution.py:206
  52.1 9.3 %collective-permute-start.2 = (s16[32,2176]{1,0:T(8,128)(2,1)S(1)}, s16[32,2176]{1,0:T(8,128)(2,1)S(1)}, u32[]{:S(2)}, u32[]{:S(2)}) collective-permute-start(s16[32,2176]{1,0:T(8,128)(2,1)S(1)} %shard_map.57), channel_id=1, source_target_pairs={{0,24},{8,16},{16,8},{24,0},{1,25},{9,17},{17,9},{25,1},{2,26},{10... | collective-permute-start | bytes 417800 | tf_op jit(solution)/shard_map/ppermute | solution.py:209
  54.9 12.9 %collective-permute-start.1 = (s16[32,2176]{1,0:T(8,128)(2,1)S(1)}, s16[32,2176]{1,0:T(8,128)(2,1)S(1)}, u32[]{:S(2)}, u32[]{:S(2)}) collective-permute-start(s16[32,2176]{1,0:T(8,128)(2,1)S(1)} %shard_map.57), channel_id=1, source_target_pairs={{0,16},{8,24},{16,0},{24,8},{1,17},{9,25},{17,1},{25,9},{2,18},{10... | collective-permute-start | bytes 417800 | tf_op jit(solution)/shard_map/ppermute | solution.py:209
  57.6 10.2 %collective-permute-start = (s16[32,2176]{1,0:T(8,128)(2,1)S(1)}, s16[32,2176]{1,0:T(8,128)(2,1)S(1)}, u32[]{:S(2)}, u32[]{:S(2)}) collective-permute-start(s16[32,2176]{1,0:T(8,128)(2,1)S(1)} %shard_map.57), channel_id=1, source_target_pairs={{0,8},{8,0},{16,24},{24,16},{1,9},{9,1},{17,25},{25,17},{2,10},{10... | collective-permute-start | bytes 417800 | tf_op jit(solution)/shard_map/ppermute | solution.py:209
  67.9 5.6 %collective-permute-start.3 = (s16[128,2176]{1,0:T(8,128)(2,1)S(1)}, s16[128,2176]{1,0:T(8,128)(2,1)S(1)}, u32[]{:S(2)}, u32[]{:S(2)}) collective-permute-start(s16[128,2176]{1,0:T(8,128)(2,1)S(1)} %pad_add_fusion.own_ref.own_code), channel_id=1, source_target_pairs={{0,1},{1,0},{2,3},{3,2},{4,5},{5,4},{6,7},{7,6},{8,9},{9,8},{10,11... | collective-permute-start | bytes 1671176 | tf_op jit(solution)/shard_map/ppermute | solution.py:210

commit v4 on v3

v4 whole, which is shorter than its diff:
```python
import functools

import jax
import jax.numpy as jnp
from jax import lax
from jax.experimental import pallas as pl
from jax.experimental.pallas import tpu as pltpu
from jax.sharding import Mesh, PartitionSpec as P

TOP = 32767.0
BASE_MAX = 6.0
DOWN_MAX = 6.0
UP_MAX = 0.5
PAIRS = 16
ROWS = 112
TILE = 128
RANKS = 8
FF = 2048
PACKED = 2 * ROWS + 16
CODE = ROWS
DOT = functools.partial(jnp.dot, preferred_element_type=jnp.float32)


def code_of(most, bound):
    root = jnp.sqrt(jnp.sqrt(most * (1.0 / bound)))
    return jnp.clip(jnp.ceil(root * TOP), 1.0, TOP)


def scale_of(code, bound):
    part = code * (1.0 / TOP)
    part = part * part
    return part * part * bound


def signed(root, values):
    root = jnp.minimum(jnp.round(root * TOP), TOP)
    return jnp.where(values < 0.0, -root, root)


def to16(values):
    return values.astype(jnp.int32).astype(jnp.int16)


def halves(values):
    high = values.astype(jnp.bfloat16)
    return high, (values - high.astype(jnp.float32)).astype(jnp.bfloat16)


def order_up_kernel(order_ref, up_ref, out_ref):
    for p in range(0, PAIRS, 4):
        rows = jnp.concatenate([up_ref[order_ref[2 * p + i]] for i in range(8)], axis=0)
        root = jnp.sqrt(jnp.sqrt(jnp.abs(rows) * (1.0 / UP_MAX)))
        out_ref[4 * p : 4 * p + 16, :] = to16(signed(root, rows))


def order_up(order, up):
    return pl.pallas_call(
        order_up_kernel,
        in_specs=[pl.BlockSpec(memory_space=pltpu.SMEM), pl.BlockSpec(memory_space=pltpu.VMEM)],
        out_specs=pl.BlockSpec(memory_space=pltpu.VMEM),
        out_shape=jax.ShapeDtypeStruct((PAIRS * 4, TILE), jnp.int16),
        compiler_params=pltpu.CompilerParams(vmem_limit_bytes=60 * 2**20),
        cost_estimate=pl.CostEstimate(flops=0, bytes_accessed=300_000, transcendentals=0),
    )(order, up)


def pack_kernel(per, order_ref, base_ref, down_ref, out_ref):
    first = pl.program_id(0) * per
    row8 = lax.broadcasted_iota(jnp.int32, (8, TILE), 0)
    lane = lax.broadcasted_iota(jnp.int32, (8, TILE), 1)
    for p in range(per):
        downs, base_codes = [], []
        for e in range(2):
            expert = order_ref[(first + p) * 2 + e]
            tile = base_ref[expert]
            size = jnp.abs(tile)
            most = jnp.max(jnp.max(size, axis=0, keepdims=True), axis=1, keepdims=True)
            code = code_of(jnp.broadcast_to(most, (1, TILE)), BASE_MAX)
            root = jnp.sqrt(size * (1.0 / scale_of(code, BASE_MAX)))
            out_ref[p, e * ROWS : (e + 1) * ROWS, :] = to16(signed(root, tile))
            base_codes.append(code)
            factor = down_ref[expert]
            most = jnp.max(jnp.abs(factor), axis=1, keepdims=True)
            code = code_of(jnp.broadcast_to(most, (RANKS, TILE)), DOWN_MAX)
            wide = jnp.concatenate([factor, jnp.zeros((RANKS, TILE - ROWS), jnp.float32)], axis=1)
            root = jnp.sqrt(jnp.abs(wide) * (1.0 / scale_of(code, DOWN_MAX)))
            downs.append(jnp.where(lane < CODE, signed(root, wide), code))
        low = (row8 & 2) == 0
        own = jnp.where(low, downs[0], pltpu.roll(downs[1], 2, 0))
        other = jnp.where(low, pltpu.roll(downs[0], 6, 0), downs[1])
        rows = jnp.concatenate([own, other], axis=0)
        lanes = jnp.concatenate([lane, lane], axis=0)
        for e in range(2):
            rows = jnp.where(lanes == CODE + 1 + e, base_codes[e], rows)
        out_ref[p, 2 * ROWS : PACKED, :] = to16(rows)


def pack(order, base, down):
    per = 4
    return pl.pallas_call(
        functools.partial(pack_kernel, per),
        grid_spec=pltpu.PrefetchScalarGridSpec(
            num_scalar_prefetch=1,
            grid=(PAIRS // per,),
            in_specs=[
                pl.BlockSpec(base.shape, lambda i, o: (0, 0, 0)),
                pl.BlockSpec(down.shape, lambda i, o: (0, 0, 0)),
            ],
            out_specs=pl.BlockSpec((per, PACKED, TILE), lambda i, o: (i, 0, 0)),
        ),
        out_shape=jax.ShapeDtypeStruct((PAIRS, PACKED, TILE), jnp.int16),
        compiler_params=pltpu.CompilerParams(vmem_limit_bytes=60 * 2**20),
        cost_estimate=pl.CostEstimate(flops=4_000_000, bytes_accessed=3_000_000, transcendentals=0),
    )(order, base, down)


def sorted_rows(rows, yb):
    i = lax.broadcasted_iota(jnp.int32, (TILE, TILE), 0)
    j = lax.broadcasted_iota(jnp.int32, (TILE, TILE), 1)
    source = (((i >> 4) & 1) << 6) | (((i >> 5) ^ yb) << 4) | (i & 15)
    pick = jnp.where(j == source, 1.0, 0.0).astype(jnp.bfloat16)
    high, low = halves(rows)
    return DOT(pick, high) + DOT(pick, low)


def merge_kernel(per, order_ref, flag_ref, place_ref, tile_ref, down_ref, own_ref, other_ref, out_ref, left_hi, left_lo):
    row, yb, core = place_ref[0], place_ref[1], place_ref[2]

    @pl.when(pl.program_id(0) == 0)
    def _():
        flags = [flag_ref[order_ref[2 * row + e]].astype(jnp.float32) for e in range(2)]
        rows = down_ref[...].astype(jnp.float32)
        cores = [rows[:, 0:8, :].reshape(TILE, TILE), rows[:, 8:16, :].reshape(TILE, TILE)]
        mine = jnp.where(core == 0, cores[0], cores[1])
        theirs = jnp.where(core == 0, cores[1], cores[0])
        expert = (lax.broadcasted_iota(jnp.int32, (TILE, TILE), 0) >> 1) & 1
        for h, factor in enumerate((mine, theirs)):
            factor = sorted_rows(factor, yb)
            scale = scale_of(factor[:, CODE : CODE + 1], DOWN_MAX) * (UP_MAX / TOP**2)
            factor = factor * jnp.abs(factor) * scale
            for e in range(2):
                part = jnp.where(expert == e, factor * flags[e], 0.0).T[0:ROWS, :]
                at = (slice(e * ROWS, (e + 1) * ROWS), slice(h * TILE, (h + 1) * TILE))
                left_hi[at], left_lo[at] = halves(part)

    ups = jnp.concatenate([jnp.concatenate([own_ref[s], other_ref[s]], axis=0) for s in range(per)], axis=1)
    ups = ups.astype(jnp.float32) * (1.0 / TOP)
    square = ups * ups
    high, low = halves(square * (ups * jnp.abs(ups)))
    delta = DOT(left_hi[...], high) + (DOT(left_lo[...], high) + DOT(left_hi[...], low))
    for s in range(per):
        codes = tile_ref[s, 2 * ROWS : PACKED, :].astype(jnp.float32)
        for e in range(2):
            scale = scale_of(codes[0:1, CODE + 1 + e : CODE + 2 + e], BASE_MAX) * (1.0 / TOP**2)
            base = tile_ref[s, e * ROWS : (e + 1) * ROWS, :].astype(jnp.float32)
            total = base * jnp.abs(base) * scale + delta[e * ROWS : (e + 1) * ROWS, s * TILE : (s + 1) * TILE]
            out_ref[e, :, s * TILE : (s + 1) * TILE] = total.astype(jnp.bfloat16)


def merge(order, flags, place, tiles, own, other):
    per = 4
    half = pl.BlockSpec((per, TILE, TILE), lambda i, *_: (i, 0, 0))
    return pl.pallas_call(
        functools.partial(merge_kernel, per),
        grid_spec=pltpu.PrefetchScalarGridSpec(
            num_scalar_prefetch=3,
            grid=(PAIRS // per,),
            in_specs=[
                pl.BlockSpec((per, PACKED, TILE), lambda i, *_: (i, 0, 0)),
                pl.BlockSpec((PAIRS, 16, TILE), lambda i, *_: (0, 2 * ROWS // 16, 0)),
                half,
                half,
            ],
            out_specs=pl.BlockSpec((2, ROWS, per * TILE), lambda i, *_: (0, 0, i)),
            scratch_shapes=[pltpu.VMEM((2 * ROWS, 2 * TILE), jnp.bfloat16)] * 2,
        ),
        out_shape=jax.ShapeDtypeStruct((2, ROWS, FF), jnp.bfloat16),
        compiler_params=pltpu.CompilerParams(vmem_limit_bytes=24 * 2**20),
        cost_estimate=pl.CostEstimate(flops=700_000_000, bytes_accessed=4_000_000, transcendentals=0),
    )(order, flags, place, tiles, tiles, own, other)


def body(base_weights, factor_down, factor_up, presence, serving_order):
    place = jnp.stack([lax.axis_index("row"), lax.axis_index("yb"), lax.axis_index("core")]).astype(jnp.int32)
    exchange = functools.partial(lax.all_to_all, split_axis=0, concat_axis=0, tiled=True)
    ups = exchange(order_up(serving_order, factor_up).reshape(PAIRS, 4, TILE), "row")
    ups = exchange(jnp.broadcast_to(ups[None], (8, PAIRS, 4, TILE)), ("ya", "xh"))
    sent = pack(serving_order, base_weights, jnp.swapaxes(factor_down, 1, 2))
    tiles = exchange(sent, "row")

    own = jnp.swapaxes(ups, 0, 1).reshape(PAIRS, 32, TILE)
    own = jnp.concatenate([own] + [lax.ppermute(own, "yb", [(i, i ^ apart) for i in range(4)]) for apart in (1, 2, 3)], axis=1)
    other = lax.ppermute(own, "core", [(0, 1), (1, 0)])
    return merge(serving_order, presence.reshape(-1), place, tiles, own, other)


def solution(mesh):
    fine = Mesh(mesh.devices.reshape(16, 2, 4, 4, 2), ("row", "ya", "yb", "xh", "core"))
    col = ("ya", "yb", "xh", "core")
    return jax.shard_map(
        body,
        mesh=fine,
        in_specs=(P(None, col, "row"), P(None, col, "row"), P(None, col, "row"), P(), P()),
        out_specs=P("row", col, None),
        check_vma=False,
    )
```

time: 81.8 us -> 83.4 us (1.020)
  the two profiles are of different devices: /device:TPU:1 before, /device:TPU:2 now
where the time goes in v4:
time: 83.4 us; the launch traced here: 82.8 us
  starting transfers between devices  28.1 us (34%)
  blocking collectives  25.3 us (30%)
  waiting for transfers between devices  18 us (22%)
  Pallas kernels  10.4 us (12%)
    all_to_all x1, blocking collectives, body(): exchange(order_up(serving_order, factor_up).reshape(PAIRS, 4, TILE), 'row')  25.3 us
    all_to_all x1, starting transfers between devices, body(): exchange(jnp.broadcast_to(ups[None], (8, PAIRS, 4, TILE)), ('ya', 'xh'))  11.6 us
    ppermute x3, starting transfers between devices, body(): lax.ppermute(own, 'yb', [(i, i ^ apart) for i in range(4)])  10.1 us
    all_to_all x1, waiting for transfers between devices, body(): exchange(jnp.broadcast_to(ups[None], (8, PAIRS, 4, TILE)), ('ya', 'xh'))  8.17 us
    pallas_call x1, Pallas kernels, pack(): pl.pallas_call(functools.partial(pack_kernel, per), grid_spec=pltpu.Prefe...  5.11 us
    all_to_all x1, starting transfers between devices, body(): tiles = exchange(sent, 'row')  4.51 us
    ppermute x3, waiting for transfers between devices, body(): lax.ppermute(own, 'yb', [(i, i ^ apart) for i in range(4)])  4.43 us
    pallas_call x1, Pallas kernels, merge(): pl.pallas_call(functools.partial(merge_kernel, per), grid_spec=pltpu.Pref...  3.87 us
  transfers between devices with their start and end apart: 6, of which 5 were waited for; matrix products, arithmetic and copies ran while one was open for 0% of the time, Pallas kernels for 6%

profile of v4, /device:TPU:2, one launch (start us, length us, event | category | flops | bytes accessed | tf_op | source)
XLA Modules:
  0.0 82.8 jit_solution(7252349875480414186)
XLA Ops:
  0.0 1.4 %shard_map.56 = s16[64,128]{1,0:T(8,128)(2,1)} custom-call(s32[32]{0:T(128)} %order_ref.5, f32[32,2,128]{2,1,0:T(2,128)} %up_ref.1), custom_call_target="tpu_custom_call" | custom-call | bytes 300000 | tf_op jit(solution)/shard_map/pallas_call | solution.py:57
  1.4 25.3 %all_to_all.15 = s16[16,4,128]{2,1,0:T(4,128)(2,1)S(1)} all-to-all(s16[16,4,128]{2,1,0:T(4,128)(2,1)} %bitcast.13), channel_id=1, replica_groups=mesh['row'=16,'ya'=2,'yb'=4,'xh'=4,'core'=2] {'row'}, dimensions={0} | all-to-all | bytes 32768 | tf_op jit(solution)/shard_map/all_to_all | solution.py:186
  26.7 0.7 broadcast_in_dim.2
  27.4 11.6 %all-to-all-start.2 = ((s16[8,16,4,128]{3,2,1,0:T(4,128)(2,1)}), s16[8,16,4,128]{3,2,1,0:T(4,128)(2,1)S(1)}, u32[]{:S(2)}, u32[]{:S(2)}) async-start(s16[8,16,4,128]{3,2,1,0:T(4,128)(2,1)} %broadcast_in_dim.2), calls=%async_computation.2 | async-start | bytes 262144 | tf_op jit(solution)/shard_map/all_to_all | solution.py:187
  39.0 5.1 %shard_map.55 = s16[16,240,128]{2,1,0:T(8,128)(2,1)} custom-call(s32[32]{0:T(128)} %order_ref.5, f32[32,112,128]{2,1,0:T(8,128)} %base_ref.1, f32[32,8,112]{2,1,0:T(8,128)} %bitcast.12), custom_call_target="tpu_custom_call" | custom-call | flops 4000000 | bytes 3000000 | tf_op jit(solution)/shard_map/pallas_call | solution.py:100
  44.1 0.0 copy-start.1
  44.1 0.0 copy-start
  44.1 8.2 %all-to-all-done.2 = s16[8,16,4,128]{3,2,1,0:T(4,128)(2,1)S(1)} async-done(((s16[8,16,4,128]{3,2,1,0:T(4,128)(2,1)}), s16[8,16,4,128]{3,2,1,0:T(4,128)(2,1)S(1)}, u32[]{:S(2)}, u32[]{:S(2)}) %all-to-all-start.2) | async-done | bytes 131104 | tf_op jit(solution)/shard_map/all_to_all | solution.py:187
  52.3 4.5 %all-to-all-start = ((s16[16,240,128]{2,1,0:T(8,128)(2,1)}), s16[16,240,128]{2,1,0:T(8,128)(2,1)S(1)}, u32[]{:S(2)}, u32[]{:S(2)}) async-start(s16[16,240,128]{2,1,0:T(8,128)(2,1)} %shard_map.55), calls=%async_computation | async-start | bytes 1966080 | tf_op jit(solution)/shard_map/all_to_all | solution.py:189
  56.8 3.2 %collective-permute-start.2 = (s16[16,32,128]{2,1,0:T(8,128)(2,1)S(1)}, s16[16,32,128]{2,1,0:T(8,128)(2,1)S(1)}, u32[]{:S(2)}, u32[]{:S(2)}) collective-permute-start(s16[16,32,128]{2,1,0:T(8,128)(2,1)S(1)} %bitcast.8), channel_id=1, source_target_pairs={{0,24},{8,16},{16,8},{24,0},{1,25},{9,17},{17,9},{25,1},{2,26},{10... | collective-permute-start | bytes 393224 | tf_op jit(solution)/shard_map/ppermute | solution.py:192
  60.0 2.9 %collective-permute-start.1 = (s16[16,32,128]{2,1,0:T(8,128)(2,1)S(1)}, s16[16,32,128]{2,1,0:T(8,128)(2,1)S(1)}, u32[]{:S(2)}, u32[]{:S(2)}) collective-permute-start(s16[16,32,128]{2,1,0:T(8,128)(2,1)S(1)} %bitcast.9), channel_id=1, source_target_pairs={{0,16},{8,24},{16,0},{24,8},{1,17},{9,25},{17,1},{25,9},{2,18},{10... | collective-permute-start | bytes 393224 | tf_op jit(solution)/shard_map/ppermute | solution.py:192
  62.9 4.0 %collective-permute-start = (s16[16,32,128]{2,1,0:T(8,128)(2,1)S(1)}, s16[16,32,128]{2,1,0:T(8,128)(2,1)S(1)}, u32[]{:S(2)}, u32[]{:S(2)}) collective-permute-start(s16[16,32,128]{2,1,0:T(8,128)(2,1)S(1)} %bitcast.10), channel_id=1, source_target_pairs={{0,8},{8,0},{16,24},{24,16},{1,9},{9,1},{17,25},{25,17},{2,10},{10... | collective-permute-start | bytes 393224 | tf_op jit(solution)/shard_map/ppermute | solution.py:192
  67.0 0.0 collective-permute-done.2
  67.0 3.4 %collective-permute-done.1 = s16[16,32,128]{2,1,0:T(8,128)(2,1)S(1)} collective-permute-done((s16[16,32,128]{2,1,0:T(8,128)(2,1)S(1)}, s16[16,32,128]{2,1,0:T(8,128)(2,1)S(1)}, u32[]{:S(2)}, u32[]{:S(2)}) %collective-permute-start.1) | collective-permute-done | bytes 131104 | tf_op jit(solution)/shard_map/ppermute | solution.py:192
  70.4 1.0 %collective-permute-done = s16[16,32,128]{2,1,0:T(8,128)(2,1)S(1)} collective-permute-done((s16[16,32,128]{2,1,0:T(8,128)(2,1)S(1)}, s16[16,32,128]{2,1,0:T(8,128)(2,1)S(1)}, u32[]{:S(2)}, u32[]{:S(2)}) %collective-permute-start) | collective-permute-done | bytes 131104 | tf_op jit(solution)/shard_map/ppermute | solution.py:192
  71.5 1.9 %collective-permute-start.3 = (s16[16,128,128]{2,1,0:T(8,128)(2,1)S(1)}, s16[16,128,128]{2,1,0:T(8,128)(2,1)S(1)}, u32[]{:S(2)}, u32[]{:S(2)}) collective-permute-start(s16[16,128,128]{2,1,0:T(8,128)(2,1)S(1)} %pad_add_fusion.own_ref), channel_id=1, source_target_pairs={{0,1},{1,0},{2,3},{3,2},{4,5},{5,4},{6,7},{7,6},{8,9},{9,8},{10,11... | collective-permute-start | bytes 1572872 | tf_op jit(solution)/shard_map/ppermute | solution.py:193
  73.4 0.0 copy-done.1
  73.4 0.1 reshape.10.flag_ref
  73.5 0.1 pad_add_fusion.1.place_ref
  73.6 1.7 %collective-permute-done.3.other_ref = s16[16,128,128]{2,1,0:T(8,128)(2,1)S(1)} collective-permute-done((s16[16,128,128]{2,1,0:T(8,128)(2,1)S(1)}, s16[16,128,128]{2,1,0:T(8,128)(2,1)S(1)}, u32[]{:S(2)}, u32[]{:S(2)}) %collective-permute-start.3) | collective-permute-done | bytes 524320 | tf_op jit(solution)/shard_map/ppermute | solution.py:193
  75.3 3.7 %all-to-all-done.tile_ref.down_ref = s16[16,240,128]{2,1,0:T(8,128)(2,1)S(1)} async-done(((s16[16,240,128]{2,1,0:T(8,128)(2,1)}), s16[16,240,128]{2,1,0:T(8,128)(2,1)S(1)}, u32[]{:S(2)}, u32[]{:S(2)}) %all-to-all-start) | async-done | bytes 983072 | tf_op jit(solution)/shard_map/all_to_all | solution.py:189
  78.9 0.0 copy-done
  79.0 3.9 %shard_map.57 = bf16[2,112,2048]{2,1,0:T(8,128)(2,1)} custom-call(s32[32]{0:T(128)S(1)} %copy-done, s32[32]{0:T(128)S(1)} %reshape.10.flag_ref, s32[3]{0:T(128)S(1)} %pad_add_fusion.1.place_ref, s16[16,240,128]{2,1,0:T(8,128)(2,1)S(1)} %all-to-all-done.tile_ref.down_ref, s16[16,240,128]{2,1,0:T(8,128)(2,1)S(1)} %all-to-all-done.tile_ref.down_ref, ...), custom_call_target="tpu_custom_call" | custom-call | flops 700000000 | bytes 4000000 | tf_op jit(solution)/shard_map/pallas_call | solution.py:163
  (2 shorter events, 0.1 us)
Async XLA Ops:
  27.4 24.9 %all-to-all-start.2 = ((s16[8,16,4,128]{3,2,1,0:T(4,128)(2,1)}), s16[8,16,4,128]{3,2,1,0:T(4,128)(2,1)S(1)}, u32[]{:S(2)}, u32[]{:S(2)}) async-start(s16[8,16,4,128]{3,2,1,0:T(4,128)(2,1)} %broadcast_in_dim.2), calls=%async_computation.2 | async-start | bytes 262144 | tf_op jit(solution)/shard_map/all_to_all | solution.py:187
  44.1 29.3 %copy-start.1 = (s32[2,16]{1,0:T(2,128)S(1)}, s32[2,16]{1,0:T(2,128)}, u32[]{:S(2)}) copy-start(s32[2,16]{1,0:T(2,128)} %param.8) | copy-start | bytes 388
  44.1 34.9 %copy-start = (s32[32]{0:T(128)S(1)}, s32[32]{0:T(128)}, u32[]{:S(2)}) copy-start(s32[32]{0:T(128)} %order_ref.5) | copy-start | bytes 388
  52.3 26.7 %all-to-all-start = ((s16[16,240,128]{2,1,0:T(8,128)(2,1)}), s16[16,240,128]{2,1,0:T(8,128)(2,1)S(1)}, u32[]{:S(2)}, u32[]{:S(2)}) async-start(s16[16,240,128]{2,1,0:T(8,128)(2,1)} %shard_map.55), calls=%async_computation | async-start | bytes 1966080 | tf_op jit(solution)/shard_map/all_to_all | solution.py:189
  56.8 10.1 %collective-permute-start.2 = (s16[16,32,128]{2,1,0:T(8,128)(2,1)S(1)}, s16[16,32,128]{2,1,0:T(8,128)(2,1)S(1)}, u32[]{:S(2)}, u32[]{:S(2)}) collective-permute-start(s16[16,32,128]{2,1,0:T(8,128)(2,1)S(1)} %bitcast.8), channel_id=1, source_target_pairs={{0,24},{8,16},{16,8},{24,0},{1,25},{9,17},{17,9},{25,1},{2,26},{10... | collective-permute-start | bytes 393224 | tf_op jit(solution)/shard_map/ppermute | solution.py:192
  60.0 10.4 %collective-permute-start.1 = (s16[16,32,128]{2,1,0:T(8,128)(2,1)S(1)}, s16[16,32,128]{2,1,0:T(8,128)(2,1)S(1)}, u32[]{:S(2)}, u32[]{:S(2)}) collective-permute-start(s16[16,32,128]{2,1,0:T(8,128)(2,1)S(1)} %bitcast.9), channel_id=1, source_target_pairs={{0,16},{8,24},{16,0},{24,8},{1,17},{9,25},{17,1},{25,9},{2,18},{10... | collective-permute-start | bytes 393224 | tf_op jit(solution)/shard_map/ppermute | solution.py:192
  62.9 8.5 %collective-permute-start = (s16[16,32,128]{2,1,0:T(8,128)(2,1)S(1)}, s16[16,32,128]{2,1,0:T(8,128)(2,1)S(1)}, u32[]{:S(2)}, u32[]{:S(2)}) collective-permute-start(s16[16,32,128]{2,1,0:T(8,128)(2,1)S(1)} %bitcast.10), channel_id=1, source_target_pairs={{0,8},{8,0},{16,24},{24,16},{1,9},{9,1},{17,25},{25,17},{2,10},{10... | collective-permute-start | bytes 393224 | tf_op jit(solution)/shard_map/ppermute | solution.py:192
  71.5 3.8 %collective-permute-start.3 = (s16[16,128,128]{2,1,0:T(8,128)(2,1)S(1)}, s16[16,128,128]{2,1,0:T(8,128)(2,1)S(1)}, u32[]{:S(2)}, u32[]{:S(2)}) collective-permute-start(s16[16,128,128]{2,1,0:T(8,128)(2,1)S(1)} %pad_add_fusion.own_ref), channel_id=1, source_target_pairs={{0,1},{1,0},{2,3},{3,2},{4,5},{5,4},{6,7},{7,6},{8,9},{9,8},{10,11... | collective-permute-start | bytes 1572872 | tf_op jit(solution)/shard_map/ppermute | solution.py:193

commit v5 on v4

--- a/solution.py
+++ b/solution.py
@@ -47,10 +47,10 @@
 
 
 def order_up_kernel(order_ref, up_ref, out_ref):
-    for p in range(0, PAIRS, 4):
-        rows = jnp.concatenate([up_ref[order_ref[2 * p + i]] for i in range(8)], axis=0)
+    for p in range(PAIRS):
+        rows = jnp.concatenate([up_ref[order_ref[2 * p]], up_ref[order_ref[2 * p + 1]]] * 2, axis=0)
         root = jnp.sqrt(jnp.sqrt(jnp.abs(rows) * (1.0 / UP_MAX)))
-        out_ref[4 * p : 4 * p + 16, :] = to16(signed(root, rows))
+        out_ref[p] = to16(jnp.concatenate([signed(root, rows)] * 4, axis=0))
 
 
 def order_up(order, up):
@@ -58,7 +58,7 @@
         order_up_kernel,
         in_specs=[pl.BlockSpec(memory_space=pltpu.SMEM), pl.BlockSpec(memory_space=pltpu.VMEM)],
         out_specs=pl.BlockSpec(memory_space=pltpu.VMEM),
-        out_shape=jax.ShapeDtypeStruct((PAIRS * 4, TILE), jnp.int16),
+        out_shape=jax.ShapeDtypeStruct((PAIRS, 32, TILE), jnp.int16),
         compiler_params=pltpu.CompilerParams(vmem_limit_bytes=60 * 2**20),
         cost_estimate=pl.CostEstimate(flops=0, bytes_accessed=300_000, transcendentals=0),
     )(order, up)
@@ -183,12 +183,11 @@
 def body(base_weights, factor_down, factor_up, presence, serving_order):
     place = jnp.stack([lax.axis_index("row"), lax.axis_index("yb"), lax.axis_index("core")]).astype(jnp.int32)
     exchange = functools.partial(lax.all_to_all, split_axis=0, concat_axis=0, tiled=True)
-    ups = exchange(order_up(serving_order, factor_up).reshape(PAIRS, 4, TILE), "row")
-    ups = exchange(jnp.broadcast_to(ups[None], (8, PAIRS, 4, TILE)), ("ya", "xh"))
+    ups = exchange(order_up(serving_order, factor_up).reshape(128, 4, TILE), ("row", "ya", "xh"))
     sent = pack(serving_order, base_weights, jnp.swapaxes(factor_down, 1, 2))
     tiles = exchange(sent, "row")
 
-    own = jnp.swapaxes(ups, 0, 1).reshape(PAIRS, 32, TILE)
+    own = ups.reshape(PAIRS, 32, TILE)
     own = jnp.concatenate([own] + [lax.ppermute(own, "yb", [(i, i ^ apart) for i in range(4)]) for apart in (1, 2, 3)], axis=1)
     other = lax.ppermute(own, "core", [(0, 1), (1, 0)])
     return merge(serving_order, presence.reshape(-1), place, tiles, own, other)

time: 83.4 us -> 79.2 us (0.950)
  the two profiles are of different devices: /device:TPU:2 before, /device:TPU:1 now
where the time goes in v5:
time: 79.2 us; the launch traced here: 78.5 us
  starting transfers between devices  47.2 us (60%)
  waiting for transfers between devices  20.6 us (26%)
  Pallas kernels  10.5 us (13%)
    all_to_all x1, starting transfers between devices, body(): exchange(order_up(serving_order, factor_up).reshape(128, 4, TILE), ('row'...  30.1 us
    all_to_all x1, waiting for transfers between devices, body(): exchange(order_up(serving_order, factor_up).reshape(128, 4, TILE), ('row'...  10.3 us
    ppermute x3, starting transfers between devices, body(): lax.ppermute(own, 'yb', [(i, i ^ apart) for i in range(4)])  9.27 us
    ppermute x3, waiting for transfers between devices, body(): lax.ppermute(own, 'yb', [(i, i ^ apart) for i in range(4)])  6.07 us
    pallas_call x1, Pallas kernels, pack(): pl.pallas_call(functools.partial(pack_kernel, per), grid_spec=pltpu.Prefe...  5.12 us
    ppermute x1, starting transfers between devices, body(): other = lax.ppermute(own, 'core', [(0, 1), (1, 0)])  4.15 us
    pallas_call x1, Pallas kernels, merge(): pl.pallas_call(functools.partial(merge_kernel, per), grid_spec=pltpu.Pref...  3.86 us
    all_to_all x1, starting transfers between devices, body(): tiles = exchange(sent, 'row')  3.64 us
  transfers between devices with their start and end apart: 6, of which 4 were waited for; matrix products, arithmetic and copies ran while one was open for 0% of the time, Pallas kernels for 7%

profile of v5, /device:TPU:1, one launch (start us, length us, event | category | flops | bytes accessed | tf_op | source)
XLA Modules:
  0.0 78.5 jit_solution(11798963281999579279)
XLA Ops:
  0.0 1.5 %shard_map.56 = s16[16,32,128]{2,1,0:T(8,128)(2,1)} custom-call(s32[32]{0:T(128)} %order_ref.5, f32[32,2,128]{2,1,0:T(2,128)} %up_ref.1), custom_call_target="tpu_custom_call" | custom-call | bytes 300000 | tf_op jit(solution)/shard_map/pallas_call | solution.py:57
  1.5 30.1 %all-to-all-start.1 = ((s16[128,4,128]{2,1,0:T(4,128)(2,1)}), s16[128,4,128]{2,1,0:T(4,128)(2,1)S(1)}, u32[]{:S(2)}, u32[]{:S(2)}) async-start(s16[128,4,128]{2,1,0:T(4,128)(2,1)} %bitcast.6), calls=%async_computation.1 | async-start | bytes 262144 | tf_op jit(solution)/shard_map/all_to_all | solution.py:186
  31.6 5.1 %shard_map.55 = s16[16,240,128]{2,1,0:T(8,128)(2,1)} custom-call(s32[32]{0:T(128)} %order_ref.5, f32[32,112,128]{2,1,0:T(8,128)} %base_ref.1, f32[32,8,112]{2,1,0:T(8,128)} %bitcast.11), custom_call_target="tpu_custom_call" | custom-call | flops 4000000 | bytes 3000000 | tf_op jit(solution)/shard_map/pallas_call | solution.py:100
  36.7 0.0 copy-start.1
  36.7 0.0 copy-start
  36.7 10.3 %all-to-all-done.1 = s16[128,4,128]{2,1,0:T(4,128)(2,1)S(1)} async-done(((s16[128,4,128]{2,1,0:T(4,128)(2,1)}), s16[128,4,128]{2,1,0:T(4,128)(2,1)S(1)}, u32[]{:S(2)}, u32[]{:S(2)}) %all-to-all-start.1) | async-done | bytes 131104 | tf_op jit(solution)/shard_map/all_to_all | solution.py:186
  47.0 3.6 %all-to-all-start = ((s16[16,240,128]{2,1,0:T(8,128)(2,1)}), s16[16,240,128]{2,1,0:T(8,128)(2,1)S(1)}, u32[]{:S(2)}, u32[]{:S(2)}) async-start(s16[16,240,128]{2,1,0:T(8,128)(2,1)} %shard_map.55), calls=%async_computation | async-start | bytes 1966080 | tf_op jit(solution)/shard_map/all_to_all | solution.py:188
  50.7 2.9 %collective-permute-start.2 = (s16[16,32,128]{2,1,0:T(8,128)(2,1)S(1)}, s16[16,32,128]{2,1,0:T(8,128)(2,1)S(1)}, u32[]{:S(2)}, u32[]{:S(2)}) collective-permute-start(s16[16,32,128]{2,1,0:T(8,128)(2,1)S(1)} %bitcast.7), channel_id=1, source_target_pairs={{0,24},{8,16},{16,8},{24,0},{1,25},{9,17},{17,9},{25,1},{2,26},{10... | collective-permute-start | bytes 393224 | tf_op jit(solution)/shard_map/ppermute | solution.py:191
  53.6 2.6 %collective-permute-start.1 = (s16[16,32,128]{2,1,0:T(8,128)(2,1)S(1)}, s16[16,32,128]{2,1,0:T(8,128)(2,1)S(1)}, u32[]{:S(2)}, u32[]{:S(2)}) collective-permute-start(s16[16,32,128]{2,1,0:T(8,128)(2,1)S(1)} %bitcast.8), channel_id=1, source_target_pairs={{0,16},{8,24},{16,0},{24,8},{1,17},{9,25},{17,1},{25,9},{2,18},{10... | collective-permute-start | bytes 393224 | tf_op jit(solution)/shard_map/ppermute | solution.py:191
  56.2 3.8 %collective-permute-start = (s16[16,32,128]{2,1,0:T(8,128)(2,1)S(1)}, s16[16,32,128]{2,1,0:T(8,128)(2,1)S(1)}, u32[]{:S(2)}, u32[]{:S(2)}) collective-permute-start(s16[16,32,128]{2,1,0:T(8,128)(2,1)S(1)} %bitcast.9), channel_id=1, source_target_pairs={{0,8},{8,0},{16,24},{24,16},{1,9},{9,1},{17,25},{25,17},{2,10},{10... | collective-permute-start | bytes 393224 | tf_op jit(solution)/shard_map/ppermute | solution.py:191
  60.0 0.0 collective-permute-done.2
  60.0 6.1 %collective-permute-done.1 = s16[16,32,128]{2,1,0:T(8,128)(2,1)S(1)} collective-permute-done((s16[16,32,128]{2,1,0:T(8,128)(2,1)S(1)}, s16[16,32,128]{2,1,0:T(8,128)(2,1)S(1)}, u32[]{:S(2)}, u32[]{:S(2)}) %collective-permute-start.1) | collective-permute-done | bytes 131104 | tf_op jit(solution)/shard_map/ppermute | solution.py:191
  66.0 0.0 collective-permute-done
  66.1 4.1 %collective-permute-start.3 = (s16[16,128,128]{2,1,0:T(8,128)(2,1)S(1)}, s16[16,128,128]{2,1,0:T(8,128)(2,1)S(1)}, u32[]{:S(2)}, u32[]{:S(2)}) collective-permute-start(s16[16,128,128]{2,1,0:T(8,128)(2,1)S(1)} %pad_add_fusion.own_ref), channel_id=1, source_target_pairs={{0,1},{1,0},{2,3},{3,2},{4,5},{5,4},{6,7},{7,6},{8,9},{9,8},{10,11... | collective-permute-start | bytes 1572872 | tf_op jit(solution)/shard_map/ppermute | solution.py:192
  70.3 0.0 copy-done.1
  70.3 0.1 reshape.9.flag_ref
  70.4 0.1 pad_add_fusion.1.place_ref
  70.4 1.3 %collective-permute-done.3.other_ref = s16[16,128,128]{2,1,0:T(8,128)(2,1)S(1)} collective-permute-done((s16[16,128,128]{2,1,0:T(8,128)(2,1)S(1)}, s16[16,128,128]{2,1,0:T(8,128)(2,1)S(1)}, u32[]{:S(2)}, u32[]{:S(2)}) %collective-permute-start.3) | collective-permute-done | bytes 524320 | tf_op jit(solution)/shard_map/ppermute | solution.py:192
  71.8 2.9 %all-to-all-done.tile_ref.down_ref = s16[16,240,128]{2,1,0:T(8,128)(2,1)S(1)} async-done(((s16[16,240,128]{2,1,0:T(8,128)(2,1)}), s16[16,240,128]{2,1,0:T(8,128)(2,1)S(1)}, u32[]{:S(2)}, u32[]{:S(2)}) %all-to-all-start) | async-done | bytes 983072 | tf_op jit(solution)/shard_map/all_to_all | solution.py:188
  74.6 0.0 copy-done
  74.7 3.9 %shard_map.57 = bf16[2,112,2048]{2,1,0:T(8,128)(2,1)} custom-call(s32[32]{0:T(128)S(1)} %copy-done, s32[32]{0:T(128)S(1)} %reshape.9.flag_ref, s32[3]{0:T(128)S(1)} %pad_add_fusion.1.place_ref, s16[16,240,128]{2,1,0:T(8,128)(2,1)S(1)} %all-to-all-done.tile_ref.down_ref, s16[16,240,128]{2,1,0:T(8,128)(2,1)S(1)} %all-to-all-done.tile_ref.down_ref, ...), custom_call_target="tpu_custom_call" | custom-call | flops 700000000 | bytes 4000000 | tf_op jit(solution)/shard_map/pallas_call | solution.py:163
  (1 shorter events, 0.0 us)
Async XLA Ops:
  1.5 45.5 %all-to-all-start.1 = ((s16[128,4,128]{2,1,0:T(4,128)(2,1)}), s16[128,4,128]{2,1,0:T(4,128)(2,1)S(1)}, u32[]{:S(2)}, u32[]{:S(2)}) async-start(s16[128,4,128]{2,1,0:T(4,128)(2,1)} %bitcast.6), calls=%async_computation.1 | async-start | bytes 262144 | tf_op jit(solution)/shard_map/all_to_all | solution.py:186
  36.7 33.5 %copy-start.1 = (s32[2,16]{1,0:T(2,128)S(1)}, s32[2,16]{1,0:T(2,128)}, u32[]{:S(2)}) copy-start(s32[2,16]{1,0:T(2,128)} %param.8) | copy-start | bytes 388
  36.7 37.9 %copy-start = (s32[32]{0:T(128)S(1)}, s32[32]{0:T(128)}, u32[]{:S(2)}) copy-start(s32[32]{0:T(128)} %order_ref.5) | copy-start | bytes 388
  47.0 27.6 %all-to-all-start = ((s16[16,240,128]{2,1,0:T(8,128)(2,1)}), s16[16,240,128]{2,1,0:T(8,128)(2,1)S(1)}, u32[]{:S(2)}, u32[]{:S(2)}) async-start(s16[16,240,128]{2,1,0:T(8,128)(2,1)} %shard_map.55), calls=%async_computation | async-start | bytes 1966080 | tf_op jit(solution)/shard_map/all_to_all | solution.py:188
  50.7 9.3 %collective-permute-start.2 = (s16[16,32,128]{2,1,0:T(8,128)(2,1)S(1)}, s16[16,32,128]{2,1,0:T(8,128)(2,1)S(1)}, u32[]{:S(2)}, u32[]{:S(2)}) collective-permute-start(s16[16,32,128]{2,1,0:T(8,128)(2,1)S(1)} %bitcast.7), channel_id=1, source_target_pairs={{0,24},{8,16},{16,8},{24,0},{1,25},{9,17},{17,9},{25,1},{2,26},{10... | collective-permute-start | bytes 393224 | tf_op jit(solution)/shard_map/ppermute | solution.py:191
  53.6 12.5 %collective-permute-start.1 = (s16[16,32,128]{2,1,0:T(8,128)(2,1)S(1)}, s16[16,32,128]{2,1,0:T(8,128)(2,1)S(1)}, u32[]{:S(2)}, u32[]{:S(2)}) collective-permute-start(s16[16,32,128]{2,1,0:T(8,128)(2,1)S(1)} %bitcast.8), channel_id=1, source_target_pairs={{0,16},{8,24},{16,0},{24,8},{1,17},{9,25},{17,1},{25,9},{2,18},{10... | collective-permute-start | bytes 393224 | tf_op jit(solution)/shard_map/ppermute | solution.py:191
  56.2 9.8 %collective-permute-start = (s16[16,32,128]{2,1,0:T(8,128)(2,1)S(1)}, s16[16,32,128]{2,1,0:T(8,128)(2,1)S(1)}, u32[]{:S(2)}, u32[]{:S(2)}) collective-permute-start(s16[16,32,128]{2,1,0:T(8,128)(2,1)S(1)} %bitcast.9), channel_id=1, source_target_pairs={{0,8},{8,0},{16,24},{24,16},{1,9},{9,1},{17,25},{25,17},{2,10},{10... | collective-permute-start | bytes 393224 | tf_op jit(solution)/shard_map/ppermute | solution.py:191
  66.1 5.7 %collective-permute-start.3 = (s16[16,128,128]{2,1,0:T(8,128)(2,1)S(1)}, s16[16,128,128]{2,1,0:T(8,128)(2,1)S(1)}, u32[]{:S(2)}, u32[]{:S(2)}) collective-permute-start(s16[16,128,128]{2,1,0:T(8,128)(2,1)S(1)} %pad_add_fusion.own_ref), channel_id=1, source_target_pairs={{0,1},{1,0},{2,3},{3,2},{4,5},{5,4},{6,7},{7,6},{8,9},{9,8},{10,11... | collective-permute-start | bytes 1572872 | tf_op jit(solution)/shard_map/ppermute | solution.py:192

commit v6 on v5

v6 whole, which is shorter than its diff:
```python
import functools

import jax
import jax.numpy as jnp
from jax import lax
from jax.experimental import pallas as pl
from jax.experimental.pallas import tpu as pltpu
from jax.sharding import Mesh, PartitionSpec as P

TOP = 32767.0
BASE_MAX = 6.0
DOWN_MAX = 6.0
UP_MAX = 0.5
PAIRS = 16
ROWS = 112
TILE = 128
RANKS = 8
FF = 2048
PACKED = 2 * ROWS + 16
CODE = ROWS
DOT = functools.partial(jnp.dot, preferred_element_type=jnp.float32)


def code_of(most, bound):
    root = jnp.sqrt(jnp.sqrt(most * (1.0 / bound)))
    return jnp.clip(jnp.ceil(root * TOP), 1.0, TOP)


def scale_of(code, bound):
    part = code * (1.0 / TOP)
    part = part * part
    return part * part * bound


def signed(root, values):
    root = jnp.minimum(jnp.round(root * TOP), TOP)
    return jnp.where(values < 0.0, -root, root)


def to16(values):
    return values.astype(jnp.int32).astype(jnp.int16)


def halves(values):
    high = values.astype(jnp.bfloat16)
    return high, (values - high.astype(jnp.float32)).astype(jnp.bfloat16)


def order_up_kernel(order_ref, up_ref, out_ref):
    for p in range(PAIRS):
        rows = jnp.concatenate([up_ref[order_ref[2 * p]], up_ref[order_ref[2 * p + 1]]] * 2, axis=0)
        root = jnp.sqrt(jnp.sqrt(jnp.abs(rows) * (1.0 / UP_MAX)))
        out_ref[p] = to16(jnp.concatenate([signed(root, rows)] * 2, axis=0))


def order_up(order, up):
    return pl.pallas_call(
        order_up_kernel,
        in_specs=[pl.BlockSpec(memory_space=pltpu.SMEM), pl.BlockSpec(memory_space=pltpu.VMEM)],
        out_specs=pl.BlockSpec(memory_space=pltpu.VMEM),
        out_shape=jax.ShapeDtypeStruct((PAIRS, 16, TILE), jnp.int16),
        compiler_params=pltpu.CompilerParams(vmem_limit_bytes=60 * 2**20),
        cost_estimate=pl.CostEstimate(flops=0, bytes_accessed=300_000, transcendentals=0),
    )(order, up)


def pack_kernel(per, order_ref, base_ref, down_ref, out_ref):
    first = pl.program_id(0) * per
    row8 = lax.broadcasted_iota(jnp.int32, (8, TILE), 0)
    lane = lax.broadcasted_iota(jnp.int32, (8, TILE), 1)
    for p in range(per):
        downs, base_codes = [], []
        for e in range(2):
            expert = order_ref[(first + p) * 2 + e]
            tile = base_ref[expert]
            size = jnp.abs(tile)
            most = jnp.max(jnp.max(size, axis=0, keepdims=True), axis=1, keepdims=True)
            code = code_of(jnp.broadcast_to(most, (1, TILE)), BASE_MAX)
            root = jnp.sqrt(size * (1.0 / scale_of(code, BASE_MAX)))
            out_ref[p, e * ROWS : (e + 1) * ROWS, :] = to16(signed(root, tile))
            base_codes.append(code)
            factor = down_ref[expert]
            most = jnp.max(jnp.abs(factor), axis=1, keepdims=True)
            code = code_of(jnp.broadcast_to(most, (RANKS, TILE)), DOWN_MAX)
            wide = jnp.concatenate([factor, jnp.zeros((RANKS, TILE - ROWS), jnp.float32)], axis=1)
            root = jnp.sqrt(jnp.abs(wide) * (1.0 / scale_of(code, DOWN_MAX)))
            downs.append(jnp.where(lane < CODE, signed(root, wide), code))
        low = (row8 & 2) == 0
        own = jnp.where(low, downs[0], pltpu.roll(downs[1], 2, 0))
        other = jnp.where(low, pltpu.roll(downs[0], 6, 0), downs[1])
        rows = jnp.concatenate([own, other], axis=0)
        lanes = jnp.concatenate([lane, lane], axis=0)
        for e in range(2):
            rows = jnp.where(lanes == CODE + 1 + e, base_codes[e], rows)
        out_ref[p, 2 * ROWS : PACKED, :] = to16(rows)


def pack(order, base, down):
    per = 4
    return pl.pallas_call(
        functools.partial(pack_kernel, per),
        grid_spec=pltpu.PrefetchScalarGridSpec(
            num_scalar_prefetch=1,
            grid=(PAIRS // per,),
            in_specs=[
                pl.BlockSpec(base.shape, lambda i, o: (0, 0, 0)),
                pl.BlockSpec(down.shape, lambda i, o: (0, 0, 0)),
            ],
            out_specs=pl.BlockSpec((per, PACKED, TILE), lambda i, o: (i, 0, 0)),
        ),
        out_shape=jax.ShapeDtypeStruct((PAIRS, PACKED, TILE), jnp.int16),
        compiler_params=pltpu.CompilerParams(vmem_limit_bytes=60 * 2**20),
        cost_estimate=pl.CostEstimate(flops=4_000_000, bytes_accessed=3_000_000, transcendentals=0),
    )(order, base, down)


def sorted_rows(rows, y, core):
    i = lax.broadcasted_iota(jnp.int32, (2 * TILE, 2 * TILE), 0)
    j = lax.broadcasted_iota(jnp.int32, (2 * TILE, 2 * TILE), 1)
    taker = jnp.where(i < 144, core, 1 - core)
    at = jnp.where(i < 32, i, jnp.where(i < 144, i - 32, i - 144))
    single = at >= 96
    apart = jnp.where(i < 32, 0, jnp.where(single, 4, (at >> 5) + 1 + 4 * taker))
    of = jnp.where(single, taker, taker ^ ((at >> 4) & 1))
    pick = jnp.where(j == ((of << 7) | ((y ^ apart) << 4) | (i & 15)), 1.0, 0.0).astype(jnp.bfloat16)
    high, low = halves(rows)
    return DOT(pick, high) + DOT(pick, low)


def merge_kernel(order_ref, flag_ref, place_ref, tile_ref, both_ref, mine_ref, other_ref, out_ref, left_hi, left_lo, done, sent):
    row, y, core = place_ref[0], place_ref[1], place_ref[2]
    rows = tile_ref[:, 2 * ROWS : PACKED, :].astype(jnp.float32)
    rows = jnp.concatenate([rows[:, 0:8, :].reshape(TILE, TILE), rows[:, 8:16, :].reshape(TILE, TILE)], axis=0)
    factor = sorted_rows(rows, y, core)
    scale = scale_of(factor[:, CODE : CODE + 1], DOWN_MAX) * (UP_MAX / TOP**2)
    factor = factor * jnp.abs(factor) * scale
    expert = (lax.broadcasted_iota(jnp.int32, (2 * TILE, TILE), 0) >> 1) & 1
    for e in range(2):
        flag = flag_ref[order_ref[2 * row + e]].astype(jnp.float32)
        part = jnp.where(expert == e, factor * flag, 0.0).T[0:ROWS, :]
        at = slice(e * ROWS, (e + 1) * ROWS)
        left_hi[at, :], left_lo[at, :] = halves(part)

    wide = 4
    for i in range(PAIRS // wide):
        spots = range(i * wide, (i + 1) * wide)
        ups = jnp.concatenate([jnp.concatenate([both_ref[s], mine_ref[s], other_ref[s]], axis=0) for s in spots], axis=1)
        ups = ups.astype(jnp.float32) * (1.0 / TOP)
        square = ups * ups
        high, low = halves(square * (ups * jnp.abs(ups)))
        delta = DOT(left_hi[...], high) + (DOT(left_lo[...], high) + DOT(left_hi[...], low))
        for at, s in enumerate(spots):
            codes = tile_ref[s, 2 * ROWS : PACKED, :].astype(jnp.float32)
            for e in range(2):
                scale = scale_of(codes[0:1, CODE + 1 + e : CODE + 2 + e], BASE_MAX) * (1.0 / TOP**2)
                base = tile_ref[s, e * ROWS : (e + 1) * ROWS, :].astype(jnp.float32)
                total = base * jnp.abs(base) * scale + delta[e * ROWS : (e + 1) * ROWS, at * TILE : (at + 1) * TILE]
                done[i, e, :, at * TILE : (at + 1) * TILE] = total.astype(jnp.bfloat16)
        pltpu.make_async_copy(done.at[i], out_ref.at[:, :, pl.ds(i * wide * TILE, wide * TILE)], sent.at[i]).start()
    for i in range(PAIRS // wide):
        pltpu.make_async_copy(done.at[i], out_ref.at[:, :, pl.ds(i * wide * TILE, wide * TILE)], sent.at[i]).wait()


def merge(order, flags, place, tiles, ups):
    wide = 4
    smem, vmem = pl.BlockSpec(memory_space=pltpu.SMEM), pl.BlockSpec(memory_space=pltpu.VMEM)
    return pl.pallas_call(
        merge_kernel,
        in_specs=[smem, smem, smem, vmem, vmem, vmem, vmem],
        out_specs=pl.BlockSpec(memory_space=pl.ANY),
        out_shape=jax.ShapeDtypeStruct((2, ROWS, FF), jnp.bfloat16),
        scratch_shapes=[
            pltpu.VMEM((2 * ROWS, 2 * TILE), jnp.bfloat16),
            pltpu.VMEM((2 * ROWS, 2 * TILE), jnp.bfloat16),
            pltpu.VMEM((PAIRS // wide, 2, ROWS, wide * TILE), jnp.bfloat16),
            pltpu.SemaphoreType.DMA((PAIRS // wide,)),
        ],
        compiler_params=pltpu.CompilerParams(vmem_limit_bytes=24 * 2**20),
        cost_estimate=pl.CostEstimate(flops=700_000_000, bytes_accessed=4_000_000, transcendentals=0),
    )(order, flags, place, tiles, *ups)


def spread(own):
    swap = [(0, 1), (1, 0)]
    far = lax.ppermute(own, "y", [(y, y ^ 4) for y in range(8)])
    both = jnp.concatenate([own, lax.ppermute(own, "core", swap)], axis=1)
    near = []
    for j in (1, 2, 3):
        pairs = [(2 * y + c, 2 * (y ^ (j + 4 * c)) + c) for y in range(8) for c in range(2)]
        near.append(lax.ppermute(both, ("y", "core"), pairs))
    mine = jnp.concatenate(near + [far], axis=1)
    return both, mine, lax.ppermute(mine, "core", swap)


def body(base_weights, factor_down, factor_up, presence, serving_order):
    place = jnp.stack([lax.axis_index("row"), lax.axis_index("y"), lax.axis_index("core")]).astype(jnp.int32)
    exchange = functools.partial(lax.all_to_all, split_axis=0, concat_axis=0, tiled=True)
    ups = exchange(order_up(serving_order, factor_up).reshape(64, 4, TILE), ("row", "xh"))
    sent = pack(serving_order, base_weights, jnp.swapaxes(factor_down, 1, 2))
    tiles = exchange(sent, "row")
    return merge(serving_order, presence.reshape(-1), place, tiles, spread(ups.reshape(PAIRS, 16, TILE)))


def solution(mesh):
    fine = Mesh(mesh.devices.reshape(16, 8, 4, 2), ("row", "y", "xh", "core"))
    col = ("y", "xh", "core")
    return jax.shard_map(
        body,
        mesh=fine,
        in_specs=(P(None, col, "row"), P(None, col, "row"), P(None, col, "row"), P(), P()),
        out_specs=P("row", col, None),
        check_vma=False,
    )
```

time: 79.2 us -> 74.2 us (0.937)
  waiting for transfers between devices: 20.6 us -> 12.8 us
  starting transfers between devices: 47.2 us -> 50.3 us
  Pallas kernels: 10.5 us -> 9.57 us
    ppermute x4 -> x6, starting transfers between devices: 13.4 us -> 23.5 us  [the longest x3 11.8 us: spread(): near.append(lax.ppermute(both, ('y', 'core'), pairs))]
    all_to_all x1, starting transfers between devices: 30.1 us -> 23.2 us  [body(): exchange(order_up(serving_order, factor_up).reshape(64, 4, TILE), ('row',...]
    all_to_all x1, waiting for transfers between devices: 10.3 us -> 5.46 us  [body(): exchange(order_up(serving_order, factor_up).reshape(64, 4, TILE), ('row',...]
    all_to_all x1, waiting for transfers between devices: 2.87 us -> 0.01 us  [body(): tiles = exchange(sent, 'row')]
    pallas_call x1, Pallas kernels: 3.86 us -> 2.96 us  [merge(): pl.pallas_call(merge_kernel, in_specs=[smem, smem, smem, vmem, vmem, vmem...]
    ppermute x4 -> x6, waiting for transfers between devices: 7.42 us -> 7.36 us  [the longest x3 5.23 us: spread(): near.append(lax.ppermute(both, ('y', 'core'), pairs))]
  transfers between devices with their start and end apart: 6 -> 8, of which waited for: 4 -> 4; matrix products, arithmetic and copies ran while one was open for 0% -> 0% of each run, Pallas kernels for 7% -> 7%
where the time goes in v6:
time: 74.2 us; the launch traced here: 73.1 us
  starting transfers between devices  50.3 us (68%)
  waiting for transfers between devices  12.8 us (17%)
  Pallas kernels  9.57 us (13%)
    all_to_all x1, starting transfers between devices, body(): exchange(order_up(serving_order, factor_up).reshape(64, 4, TILE), ('row',...  23.2 us
    ppermute x3, starting transfers between devices, spread(): near.append(lax.ppermute(both, ('y', 'core'), pairs))  11.8 us
    all_to_all x1, waiting for transfers between devices, body(): exchange(order_up(serving_order, factor_up).reshape(64, 4, TILE), ('row',...  5.46 us
    ppermute x3, waiting for transfers between devices, spread(): near.append(lax.ppermute(both, ('y', 'core'), pairs))  5.23 us
    ppermute x1, starting transfers between devices, spread(): far = lax.ppermute(own, 'y', [(y, y ^ 4) for y in range(8)])  5.21 us
    pallas_call x1, Pallas kernels, pack(): pl.pallas_call(functools.partial(pack_kernel, per), grid_spec=pltpu.Prefe...  5.13 us
    ppermute x1, starting transfers between devices, spread(): both = jnp.concatenate([own, lax.ppermute(own, 'core', swap)], axis=1)  4.01 us
    all_to_all x1, starting transfers between devices, body(): tiles = exchange(sent, 'row')  3.64 us
  transfers between devices with their start and end apart: 8, of which 4 were waited for; matrix products, arithmetic and copies ran while one was open for 0% of the time, Pallas kernels for 7%

profile of v6, /device:TPU:1, one launch (start us, length us, event | category | flops | bytes accessed | tf_op | source)
XLA Modules:
  0.0 73.1 jit_solution(2930215687835986649)
XLA Ops:
  0.0 1.5 %shard_map.56 = s16[16,16,128]{2,1,0:T(8,128)(2,1)} custom-call(s32[32]{0:T(128)} %order_ref.5, f32[32,2,128]{2,1,0:T(2,128)} %up_ref.1), custom_call_target="tpu_custom_call" | custom-call | bytes 300000 | tf_op jit(solution)/shard_map/pallas_call | solution.py:57
  1.5 23.2 %all-to-all-start.1 = ((s16[64,4,128]{2,1,0:T(4,128)(2,1)}), s16[64,4,128]{2,1,0:T(4,128)(2,1)S(1)}, u32[]{:S(2)}, u32[]{:S(2)}) async-start(s16[64,4,128]{2,1,0:T(4,128)(2,1)} %bitcast.6), calls=%async_computation.1 | async-start | bytes 131072 | tf_op jit(solution)/shard_map/all_to_all | solution.py:198
  24.6 5.1 %shard_map.55 = s16[16,240,128]{2,1,0:T(8,128)(2,1)} custom-call(s32[32]{0:T(128)} %order_ref.5, f32[32,112,128]{2,1,0:T(8,128)} %base_ref.1, f32[32,8,112]{2,1,0:T(8,128)} %bitcast.10), custom_call_target="tpu_custom_call" | custom-call | flops 4000000 | bytes 3000000 | tf_op jit(solution)/shard_map/pallas_call | solution.py:100
  29.8 0.0 copy-start.1
  29.8 0.0 copy-start
  29.8 5.5 %all-to-all-done.1 = s16[64,4,128]{2,1,0:T(4,128)(2,1)S(1)} async-done(((s16[64,4,128]{2,1,0:T(4,128)(2,1)}), s16[64,4,128]{2,1,0:T(4,128)(2,1)S(1)}, u32[]{:S(2)}, u32[]{:S(2)}) %all-to-all-start.1) | async-done | bytes 65568 | tf_op jit(solution)/shard_map/all_to_all | solution.py:198
  35.2 3.6 %all-to-all-start = ((s16[16,240,128]{2,1,0:T(8,128)(2,1)}), s16[16,240,128]{2,1,0:T(8,128)(2,1)S(1)}, u32[]{:S(2)}, u32[]{:S(2)}) async-start(s16[16,240,128]{2,1,0:T(8,128)(2,1)} %shard_map.55), calls=%async_computation | async-start | bytes 1966080 | tf_op jit(solution)/shard_map/all_to_all | solution.py:200
  38.9 4.0 %collective-permute-start = (s16[16,16,128]{2,1,0:T(8,128)(2,1)S(1)}, s16[16,16,128]{2,1,0:T(8,128)(2,1)S(1)}, u32[]{:S(2)}, u32[]{:S(2)}) collective-permute-start(s16[16,16,128]{2,1,0:T(8,128)(2,1)S(1)} %bitcast.7), channel_id=1, source_target_pairs={{0,1},{1,0},{2,3},{3,2},{4,5},{5,4},{6,7},{7,6},{8,9},{9,8},{10,11... | collective-permute-start | bytes 196616 | tf_op jit(solution)/shard_map/ppermute | solution.py:186
  42.9 0.9 %collective-permute-done = s16[16,16,128]{2,1,0:T(8,128)(2,1)S(1)} collective-permute-done((s16[16,16,128]{2,1,0:T(8,128)(2,1)S(1)}, s16[16,16,128]{2,1,0:T(8,128)(2,1)S(1)}, u32[]{:S(2)}, u32[]{:S(2)}) %collective-permute-start) | collective-permute-done | bytes 65568 | tf_op jit(solution)/shard_map/ppermute | solution.py:186
  43.8 7.2 %collective-permute-start.1 = (s16[16,32,128]{2,1,0:T(8,128)(2,1)S(1)}, s16[16,32,128]{2,1,0:T(8,128)(2,1)S(1)}, u32[]{:S(2)}, u32[]{:S(2)}) collective-permute-start(s16[16,32,128]{2,1,0:T(8,128)(2,1)S(1)} %pad_add_fusion.both_ref), channel_id=1, source_target_pairs={{0,8},{1,41},{8,0},{9,33},{16,24},{17,57},{24,16},{25,49},{32,40},... | collective-permute-start | bytes 393224 | tf_op jit(solution)/shard_map/ppermute | solution.py:190
  51.0 2.6 %collective-permute-start.2 = (s16[16,32,128]{2,1,0:T(8,128)(2,1)S(1)}, s16[16,32,128]{2,1,0:T(8,128)(2,1)S(1)}, u32[]{:S(2)}, u32[]{:S(2)}) collective-permute-start(s16[16,32,128]{2,1,0:T(8,128)(2,1)S(1)} %pad_add_fusion.both_ref), channel_id=1, source_target_pairs={{0,16},{1,49},{8,24},{9,57},{16,0},{17,33},{24,8},{25,41},{32,48},... | collective-permute-start | bytes 393224 | tf_op jit(solution)/shard_map/ppermute | solution.py:190
  53.7 5.2 %collective-permute-start.4 = (s16[16,16,128]{2,1,0:T(8,128)(2,1)S(1)}, s16[16,16,128]{2,1,0:T(8,128)(2,1)S(1)}, u32[]{:S(2)}, u32[]{:S(2)}) collective-permute-start(s16[16,16,128]{2,1,0:T(8,128)(2,1)S(1)} %bitcast.9), channel_id=1, source_target_pairs={{0,32},{8,40},{16,48},{24,56},{32,0},{40,8},{48,16},{56,24},{1,33}... | collective-permute-start | bytes 196616 | tf_op jit(solution)/shard_map/ppermute | solution.py:185
  58.9 1.9 %collective-permute-start.3 = (s16[16,32,128]{2,1,0:T(8,128)(2,1)S(1)}, s16[16,32,128]{2,1,0:T(8,128)(2,1)S(1)}, u32[]{:S(2)}, u32[]{:S(2)}) collective-permute-start(s16[16,32,128]{2,1,0:T(8,128)(2,1)S(1)} %pad_add_fusion.both_ref), channel_id=1, source_target_pairs={{0,24},{1,57},{8,16},{9,49},{16,8},{17,41},{24,0},{25,33},{32,56},... | collective-permute-start | bytes 393224 | tf_op jit(solution)/shard_map/ppermute | solution.py:190
  60.8 0.0 collective-permute-done.1
  60.9 0.0 collective-permute-done.2
  60.9 5.2 %collective-permute-done.3 = s16[16,32,128]{2,1,0:T(8,128)(2,1)S(1)} collective-permute-done((s16[16,32,128]{2,1,0:T(8,128)(2,1)S(1)}, s16[16,32,128]{2,1,0:T(8,128)(2,1)S(1)}, u32[]{:S(2)}, u32[]{:S(2)}) %collective-permute-start.3) | collective-permute-done | bytes 131104 | tf_op jit(solution)/shard_map/ppermute | solution.py:190
  66.1 0.0 collective-permute-done.4
  66.2 2.5 %collective-permute-start.5 = (s16[16,112,128]{2,1,0:T(8,128)(2,1)S(1)}, s16[16,112,128]{2,1,0:T(8,128)(2,1)S(1)}, u32[]{:S(2)}, u32[]{:S(2)}) collective-permute-start(s16[16,112,128]{2,1,0:T(8,128)(2,1)S(1)} %constant_dynamic-update-slice_fusion.mine_ref), channel_id=1, source_target_pairs={{0,1},{1,0},{2,3},{3,2},{4,5},{5,4},{6,7},{7,6},{8,9},{9,8},{10,11... | collective-permute-start | bytes 1376264 | tf_op jit(solution)/shard_map/ppermute | solution.py:192
  68.7 0.0 copy-done.1
  68.7 0.1 reshape.9.flag_ref
  68.8 0.1 pad_add_fusion.1.place_ref
  68.8 1.2 %collective-permute-done.5.other_ref = s16[16,112,128]{2,1,0:T(8,128)(2,1)S(1)} collective-permute-done((s16[16,112,128]{2,1,0:T(8,128)(2,1)S(1)}, s16[16,112,128]{2,1,0:T(8,128)(2,1)S(1)}, u32[]{:S(2)}, u32[]{:S(2)}) %collective-permute-start.5) | collective-permute-done | bytes 458784 | tf_op jit(solution)/shard_map/ppermute | solution.py:192
  70.1 0.0 all-to-all-done.tile_ref
  70.1 0.0 copy-done
  70.1 3.0 %shard_map.57 = bf16[2,112,2048]{2,1,0:T(8,128)(2,1)} custom-call(s32[32]{0:T(128)S(1)} %copy-done, s32[32]{0:T(128)S(1)} %reshape.9.flag_ref, s32[3]{0:T(128)S(1)} %pad_add_fusion.1.place_ref, s16[16,240,128]{2,1,0:T(8,128)(2,1)S(1)} %all-to-all-done.tile_ref, s16[16,32,128]{2,1,0:T(8,128)(2,1)S(1)} %pad_add_fusion.both_ref, ...), custom_call_target="tpu_custom_call" | custom-call | flops 700000000 | bytes 4000000 | tf_op jit(solution)/shard_map/pallas_call | solution.py:167
  (5 shorter events, 0.1 us)
Async XLA Ops:
  1.5 33.8 %all-to-all-start.1 = ((s16[64,4,128]{2,1,0:T(4,128)(2,1)}), s16[64,4,128]{2,1,0:T(4,128)(2,1)S(1)}, u32[]{:S(2)}, u32[]{:S(2)}) async-start(s16[64,4,128]{2,1,0:T(4,128)(2,1)} %bitcast.6), calls=%async_computation.1 | async-start | bytes 131072 | tf_op jit(solution)/shard_map/all_to_all | solution.py:198
  29.8 38.9 %copy-start.1 = (s32[2,16]{1,0:T(2,128)S(1)}, s32[2,16]{1,0:T(2,128)}, u32[]{:S(2)}) copy-start(s32[2,16]{1,0:T(2,128)} %param.8) | copy-start | bytes 388
  29.8 40.3 %copy-start = (s32[32]{0:T(128)S(1)}, s32[32]{0:T(128)}, u32[]{:S(2)}) copy-start(s32[32]{0:T(128)} %order_ref.5) | copy-start | bytes 388
  35.2 34.9 %all-to-all-start = ((s16[16,240,128]{2,1,0:T(8,128)(2,1)}), s16[16,240,128]{2,1,0:T(8,128)(2,1)S(1)}, u32[]{:S(2)}, u32[]{:S(2)}) async-start(s16[16,240,128]{2,1,0:T(8,128)(2,1)} %shard_map.55), calls=%async_computation | async-start | bytes 1966080 | tf_op jit(solution)/shard_map/all_to_all | solution.py:200
  38.9 4.9 %collective-permute-start = (s16[16,16,128]{2,1,0:T(8,128)(2,1)S(1)}, s16[16,16,128]{2,1,0:T(8,128)(2,1)S(1)}, u32[]{:S(2)}, u32[]{:S(2)}) collective-permute-start(s16[16,16,128]{2,1,0:T(8,128)(2,1)S(1)} %bitcast.7), channel_id=1, source_target_pairs={{0,1},{1,0},{2,3},{3,2},{4,5},{5,4},{6,7},{7,6},{8,9},{9,8},{10,11... | collective-permute-start | bytes 196616 | tf_op jit(solution)/shard_map/ppermute | solution.py:186
  43.8 17.0 %collective-permute-start.1 = (s16[16,32,128]{2,1,0:T(8,128)(2,1)S(1)}, s16[16,32,128]{2,1,0:T(8,128)(2,1)S(1)}, u32[]{:S(2)}, u32[]{:S(2)}) collective-permute-start(s16[16,32,128]{2,1,0:T(8,128)(2,1)S(1)} %pad_add_fusion.both_ref), channel_id=1, source_target_pairs={{0,8},{1,41},{8,0},{9,33},{16,24},{17,57},{24,16},{25,49},{32,40},... | collective-permute-start | bytes 393224 | tf_op jit(solution)/shard_map/ppermute | solution.py:190
  51.0 9.8 %collective-permute-start.2 = (s16[16,32,128]{2,1,0:T(8,128)(2,1)S(1)}, s16[16,32,128]{2,1,0:T(8,128)(2,1)S(1)}, u32[]{:S(2)}, u32[]{:S(2)}) collective-permute-start(s16[16,32,128]{2,1,0:T(8,128)(2,1)S(1)} %pad_add_fusion.both_ref), channel_id=1, source_target_pairs={{0,16},{1,49},{8,24},{9,57},{16,0},{17,33},{24,8},{25,41},{32,48},... | collective-permute-start | bytes 393224 | tf_op jit(solution)/shard_map/ppermute | solution.py:190
  53.7 12.5 %collective-permute-start.4 = (s16[16,16,128]{2,1,0:T(8,128)(2,1)S(1)}, s16[16,16,128]{2,1,0:T(8,128)(2,1)S(1)}, u32[]{:S(2)}, u32[]{:S(2)}) collective-permute-start(s16[16,16,128]{2,1,0:T(8,128)(2,1)S(1)} %bitcast.9), channel_id=1, source_target_pairs={{0,32},{8,40},{16,48},{24,56},{32,0},{40,8},{48,16},{56,24},{1,33}... | collective-permute-start | bytes 196616 | tf_op jit(solution)/shard_map/ppermute | solution.py:185
  58.9 7.2 %collective-permute-start.3 = (s16[16,32,128]{2,1,0:T(8,128)(2,1)S(1)}, s16[16,32,128]{2,1,0:T(8,128)(2,1)S(1)}, u32[]{:S(2)}, u32[]{:S(2)}) collective-permute-start(s16[16,32,128]{2,1,0:T(8,128)(2,1)S(1)} %pad_add_fusion.both_ref), channel_id=1, source_target_pairs={{0,24},{1,57},{8,16},{9,49},{16,8},{17,41},{24,0},{25,33},{32,56},... | collective-permute-start | bytes 393224 | tf_op jit(solution)/shard_map/ppermute | solution.py:190
  66.2 3.9 %collective-permute-start.5 = (s16[16,112,128]{2,1,0:T(8,128)(2,1)S(1)}, s16[16,112,128]{2,1,0:T(8,128)(2,1)S(1)}, u32[]{:S(2)}, u32[]{:S(2)}) collective-permute-start(s16[16,112,128]{2,1,0:T(8,128)(2,1)S(1)} %constant_dynamic-update-slice_fusion.mine_ref), channel_id=1, source_target_pairs={{0,1},{1,0},{2,3},{3,2},{4,5},{5,4},{6,7},{7,6},{8,9},{9,8},{10,11... | collective-permute-start | bytes 1376264 | tf_op jit(solution)/shard_map/ppermute | solution.py:192

commit v7 on v6

--- a/solution.py
+++ b/solution.py
@@ -64,39 +64,44 @@
     )(order, up)
 
 
+def rooted(part):
+    return jnp.round(part * lax.rsqrt(jnp.maximum(jnp.abs(part), 1e-30)) * TOP)
+
+
 def pack_kernel(per, order_ref, base_ref, down_ref, out_ref):
     first = pl.program_id(0) * per
     row8 = lax.broadcasted_iota(jnp.int32, (8, TILE), 0)
     lane = lax.broadcasted_iota(jnp.int32, (8, TILE), 1)
-    for p in range(per):
-        downs, base_codes = [], []
-        for e in range(2):
-            expert = order_ref[(first + p) * 2 + e]
-            tile = base_ref[expert]
-            size = jnp.abs(tile)
-            most = jnp.max(jnp.max(size, axis=0, keepdims=True), axis=1, keepdims=True)
-            code = code_of(jnp.broadcast_to(most, (1, TILE)), BASE_MAX)
-            root = jnp.sqrt(size * (1.0 / scale_of(code, BASE_MAX)))
-            out_ref[p, e * ROWS : (e + 1) * ROWS, :] = to16(signed(root, tile))
-            base_codes.append(code)
-            factor = down_ref[expert]
-            most = jnp.max(jnp.abs(factor), axis=1, keepdims=True)
-            code = code_of(jnp.broadcast_to(most, (RANKS, TILE)), DOWN_MAX)
-            wide = jnp.concatenate([factor, jnp.zeros((RANKS, TILE - ROWS), jnp.float32)], axis=1)
-            root = jnp.sqrt(jnp.abs(wide) * (1.0 / scale_of(code, DOWN_MAX)))
-            downs.append(jnp.where(lane < CODE, signed(root, wide), code))
-        low = (row8 & 2) == 0
-        own = jnp.where(low, downs[0], pltpu.roll(downs[1], 2, 0))
-        other = jnp.where(low, pltpu.roll(downs[0], 6, 0), downs[1])
-        rows = jnp.concatenate([own, other], axis=0)
-        lanes = jnp.concatenate([lane, lane], axis=0)
-        for e in range(2):
-            rows = jnp.where(lanes == CODE + 1 + e, base_codes[e], rows)
-        out_ref[p, 2 * ROWS : PACKED, :] = to16(rows)
+    experts = [order_ref[first * 2 + i] for i in range(2 * per)]
+    low = (row8 & 2) == 0
+    for h in range(0, 2 * per, 8):
+        most = [jnp.max(jnp.abs(base_ref[e]), axis=0, keepdims=True) for e in experts[h : h + 8]]
+        most = jnp.max(jnp.concatenate(most, axis=0), axis=1, keepdims=True)
+        codes = code_of(jnp.broadcast_to(most, (8, TILE)), BASE_MAX)
+        inverse = 1.0 / scale_of(codes, BASE_MAX)
+        most = [jnp.max(jnp.abs(down_ref[e]), axis=1, keepdims=True) for e in experts[h : h + 8]]
+        most = jnp.concatenate([jnp.broadcast_to(m, (RANKS, TILE)) for m in most], axis=0)
+        down_codes = code_of(most, DOWN_MAX)
+        wide = [jnp.concatenate([down_ref[e], jnp.zeros((RANKS, TILE - ROWS), jnp.float32)], axis=1) for e in experts[h : h + 8]]
+        downs = rooted(jnp.concatenate(wide, axis=0) * (1.0 / scale_of(down_codes, DOWN_MAX)))
+        lanes = lax.broadcasted_iota(jnp.int32, downs.shape, 1)
+        downs = jnp.where(lanes < CODE, downs, down_codes)
+        for i in range(8):
+            p, e = (h + i) // 2, i % 2
+            out_ref[p, e * ROWS : (e + 1) * ROWS, :] = to16(rooted(base_ref[experts[h + i]] * inverse[i : i + 1, :]))
+        for i in range(0, 8, 2):
+            even, odd = downs[8 * i : 8 * i + 8], downs[8 * i + 8 : 8 * i + 16]
+            own = jnp.where(low, even, pltpu.roll(odd, 2, 0))
+            other = jnp.where(low, pltpu.roll(even, 6, 0), odd)
+            rows = []
+            for part in (own, other):
+                part = jnp.where(lane == CODE + 1, codes[i : i + 1, :], part)
+                rows.append(jnp.where(lane == CODE + 2, codes[i + 1 : i + 2, :], part))
+            out_ref[(h + i) // 2, 2 * ROWS : PACKED, :] = to16(jnp.concatenate(rows, axis=0))
 
 
 def pack(order, base, down):
-    per = 4
+    per = 8
     return pl.pallas_call(
         functools.partial(pack_kernel, per),
         grid_spec=pltpu.PrefetchScalarGridSpec(
@@ -114,24 +119,25 @@
     )(order, base, down)
 
 
-def sorted_rows(rows, y, core):
+def sorted_rows(rows, y):
     i = lax.broadcasted_iota(jnp.int32, (2 * TILE, 2 * TILE), 0)
     j = lax.broadcasted_iota(jnp.int32, (2 * TILE, 2 * TILE), 1)
-    taker = jnp.where(i < 144, core, 1 - core)
+    taker = jnp.where(i < 144, 0, 1)
     at = jnp.where(i < 32, i, jnp.where(i < 144, i - 32, i - 144))
     single = at >= 96
-    apart = jnp.where(i < 32, 0, jnp.where(single, 4, (at >> 5) + 1 + 4 * taker))
-    of = jnp.where(single, taker, taker ^ ((at >> 4) & 1))
+    turn = at >> 5
+    apart = jnp.where(i < 32, 0, jnp.where(single, 1, jnp.where(taker == 0, 2 + turn, 7 - turn)))
+    of = jnp.where(single, taker, (at >> 4) & 1)
     pick = jnp.where(j == ((of << 7) | ((y ^ apart) << 4) | (i & 15)), 1.0, 0.0).astype(jnp.bfloat16)
     high, low = halves(rows)
     return DOT(pick, high) + DOT(pick, low)
 
 
-def merge_kernel(order_ref, flag_ref, place_ref, tile_ref, both_ref, mine_ref, other_ref, out_ref, left_hi, left_lo, done, sent):
-    row, y, core = place_ref[0], place_ref[1], place_ref[2]
+def merge_kernel(order_ref, flag_ref, place_ref, tile_ref, both_ref, fetched_ref, out_ref, left_hi, left_lo, done, sent):
+    row, y = place_ref[0], place_ref[1]
     rows = tile_ref[:, 2 * ROWS : PACKED, :].astype(jnp.float32)
     rows = jnp.concatenate([rows[:, 0:8, :].reshape(TILE, TILE), rows[:, 8:16, :].reshape(TILE, TILE)], axis=0)
-    factor = sorted_rows(rows, y, core)
+    factor = sorted_rows(rows, y)
     scale = scale_of(factor[:, CODE : CODE + 1], DOWN_MAX) * (UP_MAX / TOP**2)
     factor = factor * jnp.abs(factor) * scale
     expert = (lax.broadcasted_iota(jnp.int32, (2 * TILE, TILE), 0) >> 1) & 1
@@ -144,7 +150,7 @@
     wide = 4
     for i in range(PAIRS // wide):
         spots = range(i * wide, (i + 1) * wide)
-        ups = jnp.concatenate([jnp.concatenate([both_ref[s], mine_ref[s], other_ref[s]], axis=0) for s in spots], axis=1)
+        ups = jnp.concatenate([jnp.concatenate([both_ref[s], fetched_ref[s]], axis=0) for s in spots], axis=1)
         ups = ups.astype(jnp.float32) * (1.0 / TOP)
         square = ups * ups
         high, low = halves(square * (ups * jnp.abs(ups)))
@@ -166,7 +172,7 @@
     smem, vmem = pl.BlockSpec(memory_space=pltpu.SMEM), pl.BlockSpec(memory_space=pltpu.VMEM)
     return pl.pallas_call(
         merge_kernel,
-        in_specs=[smem, smem, smem, vmem, vmem, vmem, vmem],
+        in_specs=[smem, smem, smem, vmem, vmem, vmem],
         out_specs=pl.BlockSpec(memory_space=pl.ANY),
         out_shape=jax.ShapeDtypeStruct((2, ROWS, FF), jnp.bfloat16),
         scratch_shapes=[
@@ -181,19 +187,19 @@
 
 
 def spread(own):
-    swap = [(0, 1), (1, 0)]
-    far = lax.ppermute(own, "y", [(y, y ^ 4) for y in range(8)])
-    both = jnp.concatenate([own, lax.ppermute(own, "core", swap)], axis=1)
-    near = []
-    for j in (1, 2, 3):
-        pairs = [(2 * y + c, 2 * (y ^ (j + 4 * c)) + c) for y in range(8) for c in range(2)]
-        near.append(lax.ppermute(both, ("y", "core"), pairs))
-    mine = jnp.concatenate(near + [far], axis=1)
-    return both, mine, lax.ppermute(mine, "core", swap)
+    next_to = lax.ppermute(own, "y", [(y, y ^ 1) for y in range(8)])
+    both = lax.all_gather(own, "core", axis=1, tiled=True)
+    mine = []
+    for turn in range(3):
+        apart = (2 + turn, 7 - turn)
+        pairs = [(2 * y + c, 2 * (y ^ apart[c]) + c) for y in range(8) for c in range(2)]
+        mine.append(lax.ppermute(both, ("y", "core"), pairs))
+    mine = jnp.concatenate(mine + [next_to], axis=1)
+    return both, lax.all_gather(mine, "core", axis=1, tiled=True)
 
 
 def body(base_weights, factor_down, factor_up, presence, serving_order):
-    place = jnp.stack([lax.axis_index("row"), lax.axis_index("y"), lax.axis_index("core")]).astype(jnp.int32)
+    place = jnp.stack([lax.axis_index("row"), lax.axis_index("y")]).astype(jnp.int32)
     exchange = functools.partial(lax.all_to_all, split_axis=0, concat_axis=0, tiled=True)
     ups = exchange(order_up(serving_order, factor_up).reshape(64, 4, TILE), ("row", "xh"))
     sent = pack(serving_order, base_weights, jnp.swapaxes(factor_down, 1, 2))

time: 74.2 us -> 70.1 us (0.945)
  blocking collectives: 0 us -> 6.12 us
  starting transfers between devices: 50.3 us -> 44.5 us
  waiting for transfers between devices: 12.8 us -> 10.2 us
  Pallas kernels: 9.57 us -> 8.54 us
    all_gather x0 -> x2, blocking collectives: none -> 6.12 us  [the longest x1 3.65 us: spread(): both = lax.all_gather(own, 'core', axis=1, tiled=True)]
    ppermute x6 -> x4, starting transfers between devices: 23.5 us -> 17.7 us  [the longest x3 14.4 us: spread(): mine.append(lax.ppermute(both, ('y', 'core'), pairs))]
    ppermute x6 -> x4, waiting for transfers between devices: 7.36 us -> 3.74 us  [the longest x1 3.73 us: spread(): next_to = lax.ppermute(own, 'y', [(y, y ^ 1) for y in range(8)])]
    pallas_call x1, Pallas kernels: 5.13 us -> 4.1 us  [pack(): pl.pallas_call(functools.partial(pack_kernel, per), grid_spec=pltpu.Prefe...]
    all_to_all x1, waiting for transfers between devices: 5.46 us -> 6.47 us  [body(): exchange(order_up(serving_order, factor_up).reshape(64, 4, TILE), ('row',...]
  transfers between devices with their start and end apart: 8 -> 6, of which waited for: 4 -> 2; matrix products, arithmetic and copies ran while one was open for 0% -> 0% of each run, Pallas kernels for 7% -> 6%
where the time goes in v7:
time: 70.1 us; the launch traced here: 69.7 us
  starting transfers between devices  44.5 us (63%)
  waiting for transfers between devices  10.2 us (15%)
  Pallas kernels  8.54 us (12%)
  blocking collectives  6.12 us (9%)
    all_to_all x1, starting transfers between devices, body(): exchange(order_up(serving_order, factor_up).reshape(64, 4, TILE), ('row',...  23.2 us
    ppermute x3, starting transfers between devices, spread(): mine.append(lax.ppermute(both, ('y', 'core'), pairs))  14.4 us
    all_to_all x1, waiting for transfers between devices, body(): exchange(order_up(serving_order, factor_up).reshape(64, 4, TILE), ('row',...  6.47 us
    pallas_call x1, Pallas kernels, pack(): pl.pallas_call(functools.partial(pack_kernel, per), grid_spec=pltpu.Prefe...  4.1 us
    ppermute x1, waiting for transfers between devices, spread(): next_to = lax.ppermute(own, 'y', [(y, y ^ 1) for y in range(8)])  3.73 us
    all_gather x1, blocking collectives, spread(): both = lax.all_gather(own, 'core', axis=1, tiled=True)  3.65 us
    all_to_all x1, starting transfers between devices, body(): tiles = exchange(sent, 'row')  3.64 us
    ppermute x1, starting transfers between devices, spread(): next_to = lax.ppermute(own, 'y', [(y, y ^ 1) for y in range(8)])  3.31 us
  transfers between devices with their start and end apart: 6, of which 2 were waited for; matrix products, arithmetic and copies ran while one was open for 0% of the time, Pallas kernels for 6%

profile of v7, /device:TPU:1, one launch (start us, length us, event | category | flops | bytes accessed | tf_op | source)
XLA Modules:
  0.0 69.7 jit_solution(2788709377649933193)
XLA Ops:
  0.0 1.5 %shard_map.56 = s16[16,16,128]{2,1,0:T(8,128)(2,1)} custom-call(s32[32]{0:T(128)} %order_ref.5, f32[32,2,128]{2,1,0:T(2,128)} %up_ref.1), custom_call_target="tpu_custom_call" | custom-call | bytes 300000 | tf_op jit(solution)/shard_map/pallas_call | solution.py:57
  1.5 23.2 %all-to-all-start.1 = ((s16[64,4,128]{2,1,0:T(4,128)(2,1)}), s16[64,4,128]{2,1,0:T(4,128)(2,1)S(1)}, u32[]{:S(2)}, u32[]{:S(2)}) async-start(s16[64,4,128]{2,1,0:T(4,128)(2,1)} %bitcast.7), calls=%async_computation.1 | async-start | bytes 131072 | tf_op jit(solution)/shard_map/all_to_all | solution.py:204
  24.6 0.0 copy-start.1
  24.7 4.1 %shard_map.55 = s16[16,240,128]{2,1,0:T(8,128)(2,1)} custom-call(s32[32]{0:T(128)} %order_ref.5, f32[32,112,128]{2,1,0:T(8,128)} %base_ref.1, f32[32,8,112]{2,1,0:T(8,128)} %bitcast.8), custom_call_target="tpu_custom_call" | custom-call | flops 4000000 | bytes 3000000 | tf_op jit(solution)/shard_map/pallas_call | solution.py:105
  28.8 0.0 copy-start
  28.8 6.5 %all-to-all-done.1 = s16[64,4,128]{2,1,0:T(4,128)(2,1)S(1)} async-done(((s16[64,4,128]{2,1,0:T(4,128)(2,1)}), s16[64,4,128]{2,1,0:T(4,128)(2,1)S(1)}, u32[]{:S(2)}, u32[]{:S(2)}) %all-to-all-start.1) | async-done | bytes 65568 | tf_op jit(solution)/shard_map/all_to_all | solution.py:204
  35.2 3.6 %all-to-all-start = ((s16[16,240,128]{2,1,0:T(8,128)(2,1)}), s16[16,240,128]{2,1,0:T(8,128)(2,1)S(1)}, u32[]{:S(2)}, u32[]{:S(2)}) async-start(s16[16,240,128]{2,1,0:T(8,128)(2,1)} %shard_map.55), calls=%async_computation | async-start | bytes 1966080 | tf_op jit(solution)/shard_map/all_to_all | solution.py:206
  38.9 3.7 %all_gather.6.both_ref = s16[16,32,128]{2,1,0:T(8,128)(2,1)S(1)} all-gather(s16[16,16,128]{2,1,0:T(8,128)(2,1)S(1)} %bitcast.5), channel_id=1, replica_groups=mesh['row'=16,'y'=8,'xh'=4,'core'=2] {'core'}, dimensions={1}, use_global_device_ids=true | all-gather | bytes 196608 | tf_op jit(solution)/shard_map/all_gather | solution.py:191
  42.5 7.2 %collective-permute-start.2 = (s16[16,32,128]{2,1,0:T(8,128)(2,1)S(1)}, s16[16,32,128]{2,1,0:T(8,128)(2,1)S(1)}, u32[]{:S(2)}, u32[]{:S(2)}) collective-permute-start(s16[16,32,128]{2,1,0:T(8,128)(2,1)S(1)} %all_gather.6.both_ref), channel_id=1, source_target_pairs={{0,32},{1,41},{8,40},{9,33},{16,48},{17,57},{24,56},{25,49},{32,0}... | collective-permute-start | bytes 393224 | tf_op jit(solution)/shard_map/ppermute | solution.py:196
  49.8 2.6 %collective-permute-start.1 = (s16[16,32,128]{2,1,0:T(8,128)(2,1)S(1)}, s16[16,32,128]{2,1,0:T(8,128)(2,1)S(1)}, u32[]{:S(2)}, u32[]{:S(2)}) collective-permute-start(s16[16,32,128]{2,1,0:T(8,128)(2,1)S(1)} %all_gather.6.both_ref), channel_id=1, source_target_pairs={{0,24},{1,49},{8,16},{9,57},{16,8},{17,33},{24,0},{25,41},{32,56},... | collective-permute-start | bytes 393224 | tf_op jit(solution)/shard_map/ppermute | solution.py:196
  52.4 4.5 %collective-permute-start = (s16[16,32,128]{2,1,0:T(8,128)(2,1)S(1)}, s16[16,32,128]{2,1,0:T(8,128)(2,1)S(1)}, u32[]{:S(2)}, u32[]{:S(2)}) collective-permute-start(s16[16,32,128]{2,1,0:T(8,128)(2,1)S(1)} %all_gather.6.both_ref), channel_id=1, source_target_pairs={{0,16},{1,57},{8,24},{9,49},{16,0},{17,41},{24,8},{25,33},{32,48},... | collective-permute-start | bytes 393224 | tf_op jit(solution)/shard_map/ppermute | solution.py:196
  57.0 0.0 copy-done.1
  57.0 0.1 reshape.9.flag_ref
  57.0 3.3 %collective-permute-start.3 = (s16[16,16,128]{2,1,0:T(8,128)(2,1)S(1)}, s16[16,16,128]{2,1,0:T(8,128)(2,1)S(1)}, u32[]{:S(2)}, u32[]{:S(2)}) collective-permute-start(s16[16,16,128]{2,1,0:T(8,128)(2,1)S(1)} %bitcast.6), channel_id=1, source_target_pairs={{0,8},{8,0},{16,24},{24,16},{32,40},{40,32},{48,56},{56,48},{1,9},... | collective-permute-start | bytes 196616 | tf_op jit(solution)/shard_map/ppermute | solution.py:190
  60.4 0.1 pad_add_fusion.1.place_ref
  60.4 3.7 %collective-permute-done.3 = s16[16,16,128]{2,1,0:T(8,128)(2,1)S(1)} collective-permute-done((s16[16,16,128]{2,1,0:T(8,128)(2,1)S(1)}, s16[16,16,128]{2,1,0:T(8,128)(2,1)S(1)}, u32[]{:S(2)}, u32[]{:S(2)}) %collective-permute-start.3) | collective-permute-done | bytes 65568 | tf_op jit(solution)/shard_map/ppermute | solution.py:190
  64.2 0.0 collective-permute-done.2
  64.2 0.0 collective-permute-done.1
  64.2 0.0 collective-permute-done
  64.2 2.5 %all_gather.7.fetched_ref = s16[16,224,128]{2,1,0:T(8,128)(2,1)S(1)} all-gather(s16[16,112,128]{2,1,0:T(8,128)(2,1)S(1)} %pad_add_fusion), channel_id=1, replica_groups=mesh['row'=16,'y'=8,'xh'=4,'core'=2] {'core'}, dimensions={1}, use_global_device_ids=true | all-gather | bytes 1376256 | tf_op jit(solution)/shard_map/all_gather | solution.py:198
  66.7 0.0 all-to-all-done.tile_ref
  66.7 0.0 copy-done
  66.7 3.0 %shard_map.57 = bf16[2,112,2048]{2,1,0:T(8,128)(2,1)} custom-call(s32[32]{0:T(128)S(1)} %copy-done, s32[32]{0:T(128)S(1)} %reshape.9.flag_ref, s32[2]{0:T(128)S(1)} %pad_add_fusion.1.place_ref, s16[16,240,128]{2,1,0:T(8,128)(2,1)S(1)} %all-to-all-done.tile_ref, s16[16,32,128]{2,1,0:T(8,128)(2,1)S(1)} %all_gather.6.both_ref, ...), custom_call_target="tpu_custom_call" | custom-call | flops 700000000 | bytes 4000000 | tf_op jit(solution)/shard_map/pallas_call | solution.py:173
  (1 shorter events, 0.0 us)
Async XLA Ops:
  1.5 33.8 %all-to-all-start.1 = ((s16[64,4,128]{2,1,0:T(4,128)(2,1)}), s16[64,4,128]{2,1,0:T(4,128)(2,1)S(1)}, u32[]{:S(2)}, u32[]{:S(2)}) async-start(s16[64,4,128]{2,1,0:T(4,128)(2,1)} %bitcast.7), calls=%async_computation.1 | async-start | bytes 131072 | tf_op jit(solution)/shard_map/all_to_all | solution.py:204
  24.6 32.3 %copy-start.1 = (s32[2,16]{1,0:T(2,128)S(1)}, s32[2,16]{1,0:T(2,128)}, u32[]{:S(2)}) copy-start(s32[2,16]{1,0:T(2,128)} %param.8) | copy-start | bytes 388
  28.8 37.9 %copy-start = (s32[32]{0:T(128)S(1)}, s32[32]{0:T(128)}, u32[]{:S(2)}) copy-start(s32[32]{0:T(128)} %order_ref.5) | copy-start | bytes 388
  35.2 31.5 %all-to-all-start = ((s16[16,240,128]{2,1,0:T(8,128)(2,1)}), s16[16,240,128]{2,1,0:T(8,128)(2,1)S(1)}, u32[]{:S(2)}, u32[]{:S(2)}) async-start(s16[16,240,128]{2,1,0:T(8,128)(2,1)} %shard_map.55), calls=%async_computation | async-start | bytes 1966080 | tf_op jit(solution)/shard_map/all_to_all | solution.py:206
  42.5 21.6 %collective-permute-start.2 = (s16[16,32,128]{2,1,0:T(8,128)(2,1)S(1)}, s16[16,32,128]{2,1,0:T(8,128)(2,1)S(1)}, u32[]{:S(2)}, u32[]{:S(2)}) collective-permute-start(s16[16,32,128]{2,1,0:T(8,128)(2,1)S(1)} %all_gather.6.both_ref), channel_id=1, source_target_pairs={{0,32},{1,41},{8,40},{9,33},{16,48},{17,57},{24,56},{25,49},{32,0}... | collective-permute-start | bytes 393224 | tf_op jit(solution)/shard_map/ppermute | solution.py:196
  49.8 14.4 %collective-permute-start.1 = (s16[16,32,128]{2,1,0:T(8,128)(2,1)S(1)}, s16[16,32,128]{2,1,0:T(8,128)(2,1)S(1)}, u32[]{:S(2)}, u32[]{:S(2)}) collective-permute-start(s16[16,32,128]{2,1,0:T(8,128)(2,1)S(1)} %all_gather.6.both_ref), channel_id=1, source_target_pairs={{0,24},{1,49},{8,16},{9,57},{16,8},{17,33},{24,0},{25,41},{32,56},... | collective-permute-start | bytes 393224 | tf_op jit(solution)/shard_map/ppermute | solution.py:196
  52.4 11.8 %collective-permute-start = (s16[16,32,128]{2,1,0:T(8,128)(2,1)S(1)}, s16[16,32,128]{2,1,0:T(8,128)(2,1)S(1)}, u32[]{:S(2)}, u32[]{:S(2)}) collective-permute-start(s16[16,32,128]{2,1,0:T(8,128)(2,1)S(1)} %all_gather.6.both_ref), channel_id=1, source_target_pairs={{0,16},{1,57},{8,24},{9,49},{16,0},{17,41},{24,8},{25,33},{32,48},... | collective-permute-start | bytes 393224 | tf_op jit(solution)/shard_map/ppermute | solution.py:196
  57.0 7.1 %collective-permute-start.3 = (s16[16,16,128]{2,1,0:T(8,128)(2,1)S(1)}, s16[16,16,128]{2,1,0:T(8,128)(2,1)S(1)}, u32[]{:S(2)}, u32[]{:S(2)}) collective-permute-start(s16[16,16,128]{2,1,0:T(8,128)(2,1)S(1)} %bitcast.6), channel_id=1, source_target_pairs={{0,8},{8,0},{16,24},{24,16},{32,40},{40,32},{48,56},{56,48},{1,9},... | collective-permute-start | bytes 196616 | tf_op jit(solution)/shard_map/ppermute | solution.py:190

commit v8 on v7

--- a/solution.py
+++ b/solution.py
@@ -68,7 +68,7 @@
     return jnp.round(part * lax.rsqrt(jnp.maximum(jnp.abs(part), 1e-30)) * TOP)
 
 
-def pack_kernel(per, order_ref, base_ref, down_ref, out_ref):
+def pack_kernel(per, order_ref, flag_ref, base_ref, down_ref, out_ref):
     first = pl.program_id(0) * per
     row8 = lax.broadcasted_iota(jnp.int32, (8, TILE), 0)
     lane = lax.broadcasted_iota(jnp.int32, (8, TILE), 1)
@@ -82,7 +82,8 @@
         most = [jnp.max(jnp.abs(down_ref[e]), axis=1, keepdims=True) for e in experts[h : h + 8]]
         most = jnp.concatenate([jnp.broadcast_to(m, (RANKS, TILE)) for m in most], axis=0)
         down_codes = code_of(most, DOWN_MAX)
-        wide = [jnp.concatenate([down_ref[e], jnp.zeros((RANKS, TILE - ROWS), jnp.float32)], axis=1) for e in experts[h : h + 8]]
+        flags = [flag_ref[e >> 4, e & 15].astype(jnp.float32) for e in experts[h : h + 8]]
+        wide = [jnp.concatenate([down_ref[e] * f, jnp.zeros((RANKS, TILE - ROWS), jnp.float32)], axis=1) for e, f in zip(experts[h : h + 8], flags)]
         downs = rooted(jnp.concatenate(wide, axis=0) * (1.0 / scale_of(down_codes, DOWN_MAX)))
         lanes = lax.broadcasted_iota(jnp.int32, downs.shape, 1)
         downs = jnp.where(lanes < CODE, downs, down_codes)
@@ -100,26 +101,26 @@
             out_ref[(h + i) // 2, 2 * ROWS : PACKED, :] = to16(jnp.concatenate(rows, axis=0))
 
 
-def pack(order, base, down):
+def pack(order, flags, base, down):
     per = 8
     return pl.pallas_call(
         functools.partial(pack_kernel, per),
         grid_spec=pltpu.PrefetchScalarGridSpec(
-            num_scalar_prefetch=1,
+            num_scalar_prefetch=2,
             grid=(PAIRS // per,),
             in_specs=[
-                pl.BlockSpec(base.shape, lambda i, o: (0, 0, 0)),
-                pl.BlockSpec(down.shape, lambda i, o: (0, 0, 0)),
+                pl.BlockSpec(base.shape, lambda i, *_: (0, 0, 0)),
+                pl.BlockSpec(down.shape, lambda i, *_: (0, 0, 0)),
             ],
-            out_specs=pl.BlockSpec((per, PACKED, TILE), lambda i, o: (i, 0, 0)),
+            out_specs=pl.BlockSpec((per, PACKED, TILE), lambda i, *_: (i, 0, 0)),
         ),
         out_shape=jax.ShapeDtypeStruct((PAIRS, PACKED, TILE), jnp.int16),
         compiler_params=pltpu.CompilerParams(vmem_limit_bytes=60 * 2**20),
         cost_estimate=pl.CostEstimate(flops=4_000_000, bytes_accessed=3_000_000, transcendentals=0),
-    )(order, base, down)
-
-
-def sorted_rows(rows, y):
+    )(order, flags, base, down)
+
+
+def sorter(y):
     i = lax.broadcasted_iota(jnp.int32, (2 * TILE, 2 * TILE), 0)
     j = lax.broadcasted_iota(jnp.int32, (2 * TILE, 2 * TILE), 1)
     taker = jnp.where(i < 144, 0, 1)
@@ -128,22 +129,19 @@
     turn = at >> 5
     apart = jnp.where(i < 32, 0, jnp.where(single, 1, jnp.where(taker == 0, 2 + turn, 7 - turn)))
     of = jnp.where(single, taker, (at >> 4) & 1)
-    pick = jnp.where(j == ((of << 7) | ((y ^ apart) << 4) | (i & 15)), 1.0, 0.0).astype(jnp.bfloat16)
-    high, low = halves(rows)
-    return DOT(pick, high) + DOT(pick, low)
-
-
-def merge_kernel(order_ref, flag_ref, place_ref, tile_ref, both_ref, fetched_ref, out_ref, left_hi, left_lo, done, sent):
-    row, y = place_ref[0], place_ref[1]
+    return jnp.where(j == ((of << 7) | ((y ^ apart) << 4) | (i & 15)), 1.0, 0.0).astype(jnp.bfloat16)
+
+
+def merge_kernel(pick_ref, tile_ref, both_ref, fetched_ref, out_ref, left_hi, left_lo, done, sent):
     rows = tile_ref[:, 2 * ROWS : PACKED, :].astype(jnp.float32)
     rows = jnp.concatenate([rows[:, 0:8, :].reshape(TILE, TILE), rows[:, 8:16, :].reshape(TILE, TILE)], axis=0)
-    factor = sorted_rows(rows, y)
+    high, low = halves(rows)
+    factor = DOT(pick_ref[...], high) + DOT(pick_ref[...], low)
     scale = scale_of(factor[:, CODE : CODE + 1], DOWN_MAX) * (UP_MAX / TOP**2)
     factor = factor * jnp.abs(factor) * scale
     expert = (lax.broadcasted_iota(jnp.int32, (2 * TILE, TILE), 0) >> 1) & 1
     for e in range(2):
-        flag = flag_ref[order_ref[2 * row + e]].astype(jnp.float32)
-        part = jnp.where(expert == e, factor * flag, 0.0).T[0:ROWS, :]
+        part = jnp.where(expert == e, factor, 0.0).T[0:ROWS, :]
         at = slice(e * ROWS, (e + 1) * ROWS)
         left_hi[at, :], left_lo[at, :] = halves(part)
 
@@ -167,12 +165,11 @@
         pltpu.make_async_copy(done.at[i], out_ref.at[:, :, pl.ds(i * wide * TILE, wide * TILE)], sent.at[i]).wait()
 
 
-def merge(order, flags, place, tiles, ups):
+def merge(pick, tiles, ups):
     wide = 4
-    smem, vmem = pl.BlockSpec(memory_space=pltpu.SMEM), pl.BlockSpec(memory_space=pltpu.VMEM)
     return pl.pallas_call(
         merge_kernel,
-        in_specs=[smem, smem, smem, vmem, vmem, vmem],
+        in_specs=[pl.BlockSpec(memory_space=pltpu.VMEM)] * 4,
         out_specs=pl.BlockSpec(memory_space=pl.ANY),
         out_shape=jax.ShapeDtypeStruct((2, ROWS, FF), jnp.bfloat16),
         scratch_shapes=[
@@ -183,7 +180,7 @@
         ],
         compiler_params=pltpu.CompilerParams(vmem_limit_bytes=24 * 2**20),
         cost_estimate=pl.CostEstimate(flops=700_000_000, bytes_accessed=4_000_000, transcendentals=0),
-    )(order, flags, place, tiles, *ups)
+    )(pick, tiles, *ups)
 
 
 def spread(own):
@@ -199,12 +196,11 @@
 
 
 def body(base_weights, factor_down, factor_up, presence, serving_order):
-    place = jnp.stack([lax.axis_index("row"), lax.axis_index("y")]).astype(jnp.int32)
     exchange = functools.partial(lax.all_to_all, split_axis=0, concat_axis=0, tiled=True)
     ups = exchange(order_up(serving_order, factor_up).reshape(64, 4, TILE), ("row", "xh"))
-    sent = pack(serving_order, base_weights, jnp.swapaxes(factor_down, 1, 2))
+    sent = pack(serving_order, presence, base_weights, jnp.swapaxes(factor_down, 1, 2))
     tiles = exchange(sent, "row")
-    return merge(serving_order, presence.reshape(-1), place, tiles, spread(ups.reshape(PAIRS, 16, TILE)))
+    return merge(sorter(lax.axis_index("y")), tiles, spread(ups.reshape(PAIRS, 16, TILE)))
 
 
 def solution(mesh):

time: 70.1 us -> 71.6 us (1.021)
  waiting for transfers between devices: 10.2 us -> 11.8 us
  blocking collectives: 6.12 us -> 7.29 us
  starting transfers between devices: 44.5 us -> 43.6 us
    ppermute x3, waiting for transfers between devices: 0.01 us -> 5.24 us  [spread(): mine.append(lax.ppermute(both, ('y', 'core'), pairs))]
    ppermute x1, waiting for transfers between devices: 3.73 us -> 0.01 us  [spread(): next_to = lax.ppermute(own, 'y', [(y, y ^ 1) for y in range(8)])]
    ppermute x3, starting transfers between devices: 14.4 us -> 13.5 us  [spread(): mine.append(lax.ppermute(both, ('y', 'core'), pairs))]
    all_gather x1, blocking collectives: 2.46 us -> 3.35 us  [spread(): return (both, lax.all_gather(mine, 'core', axis=1, tiled=True))]
  transfers between devices with their start and end apart: 6 -> 6, of which waited for: 2 -> 3; matrix products, arithmetic and copies ran while one was open for 0% -> 1% of each run, Pallas kernels for 6% -> 6%
where the time goes in v8:
time: 71.6 us; the launch traced here: 71.1 us
  starting transfers between devices  43.6 us (61%)
  waiting for transfers between devices  11.8 us (16%)
  Pallas kernels  7.88 us (11%)
  blocking collectives  7.29 us (10%)
    all_to_all x1, starting transfers between devices, body(): exchange(order_up(serving_order, factor_up).reshape(64, 4, TILE), ('row',...  23.2 us
    ppermute x3, starting transfers between devices, spread(): mine.append(lax.ppermute(both, ('y', 'core'), pairs))  13.5 us
    all_to_all x1, waiting for transfers between devices, body(): exchange(order_up(serving_order, factor_up).reshape(64, 4, TILE), ('row',...  6.58 us
    ppermute x3, waiting for transfers between devices, spread(): mine.append(lax.ppermute(both, ('y', 'core'), pairs))  5.24 us
    pallas_call x1, Pallas kernels, pack(): pl.pallas_call(functools.partial(pack_kernel, per), grid_spec=pltpu.Prefe...  4.01 us
    all_gather x1, blocking collectives, spread(): both = lax.all_gather(own, 'core', axis=1, tiled=True)  3.93 us
    all_to_all x1, starting transfers between devices, body(): tiles = exchange(sent, 'row')  3.64 us
    all_gather x1, blocking collectives, spread(): return (both, lax.all_gather(mine, 'core', axis=1, tiled=True))  3.35 us
  transfers between devices with their start and end apart: 6, of which 3 were waited for; matrix products, arithmetic and copies ran while one was open for 1% of the time, Pallas kernels for 6%

profile of v8, /device:TPU:1, one launch (start us, length us, event | category | flops | bytes accessed | tf_op | source)
XLA Modules:
  0.0 71.1 jit_solution(14833321305220861282)
XLA Ops:
  0.0 1.5 %shard_map.56 = s16[16,16,128]{2,1,0:T(8,128)(2,1)} custom-call(s32[32]{0:T(128)} %order_ref.3, f32[32,2,128]{2,1,0:T(2,128)} %up_ref.1), custom_call_target="tpu_custom_call" | custom-call | bytes 300000 | tf_op jit(solution)/shard_map/pallas_call | solution.py:57
  1.5 23.2 %all-to-all-start.1 = ((s16[64,4,128]{2,1,0:T(4,128)(2,1)}), s16[64,4,128]{2,1,0:T(4,128)(2,1)S(1)}, u32[]{:S(2)}, u32[]{:S(2)}) async-start(s16[64,4,128]{2,1,0:T(4,128)(2,1)} %bitcast.5), calls=%async_computation.1 | async-start | bytes 131072 | tf_op jit(solution)/shard_map/all_to_all | solution.py:200
  24.6 4.0 %shard_map.55 = s16[16,240,128]{2,1,0:T(8,128)(2,1)} custom-call(s32[32]{0:T(128)} %order_ref.3, s32[2,16]{1,0:T(2,128)} %flag_ref.1, f32[32,112,128]{2,1,0:T(8,128)} %base_ref.1, f32[32,8,112]{2,1,0:T(8,128)} %bitcast.6), custom_call_target="tpu_custom_call" | custom-call | flops 4000000 | bytes 3000000 | tf_op jit(solution)/shard_map/pallas_call | solution.py:106
  28.7 6.6 %all-to-all-done.1 = s16[64,4,128]{2,1,0:T(4,128)(2,1)S(1)} async-done(((s16[64,4,128]{2,1,0:T(4,128)(2,1)}), s16[64,4,128]{2,1,0:T(4,128)(2,1)S(1)}, u32[]{:S(2)}, u32[]{:S(2)}) %all-to-all-start.1) | async-done | bytes 65568 | tf_op jit(solution)/shard_map/all_to_all | solution.py:200
  35.2 3.6 %all-to-all-start = ((s16[16,240,128]{2,1,0:T(8,128)(2,1)}), s16[16,240,128]{2,1,0:T(8,128)(2,1)S(1)}, u32[]{:S(2)}, u32[]{:S(2)}) async-start(s16[16,240,128]{2,1,0:T(8,128)(2,1)} %shard_map.55), calls=%async_computation | async-start | bytes 1966080 | tf_op jit(solution)/shard_map/all_to_all | solution.py:202
  38.9 3.3 %collective-permute-start.3 = (s16[16,16,128]{2,1,0:T(8,128)(2,1)S(1)}, s16[16,16,128]{2,1,0:T(8,128)(2,1)S(1)}, u32[]{:S(2)}, u32[]{:S(2)}) collective-permute-start(s16[16,16,128]{2,1,0:T(8,128)(2,1)S(1)} %bitcast.3), channel_id=1, source_target_pairs={{0,8},{8,0},{16,24},{24,16},{32,40},{40,32},{48,56},{56,48},{1,9},... | collective-permute-start | bytes 196616 | tf_op jit(solution)/shard_map/ppermute | solution.py:187
  42.3 3.9 %all_gather.6.both_ref = s16[16,32,128]{2,1,0:T(8,128)(2,1)S(1)} all-gather(s16[16,16,128]{2,1,0:T(8,128)(2,1)S(1)} %bitcast.4), channel_id=1, replica_groups=mesh['row'=16,'y'=8,'xh'=4,'core'=2] {'core'}, dimensions={1}, use_global_device_ids=true | all-gather | bytes 196608 | tf_op jit(solution)/shard_map/all_gather | solution.py:188
  46.2 6.8 %collective-permute-start.2 = (s16[16,32,128]{2,1,0:T(8,128)(2,1)S(1)}, s16[16,32,128]{2,1,0:T(8,128)(2,1)S(1)}, u32[]{:S(2)}, u32[]{:S(2)}) collective-permute-start(s16[16,32,128]{2,1,0:T(8,128)(2,1)S(1)} %all_gather.6.both_ref), channel_id=1, source_target_pairs={{0,32},{1,41},{8,40},{9,33},{16,48},{17,57},{24,56},{25,49},{32,0}... | collective-permute-start | bytes 393224 | tf_op jit(solution)/shard_map/ppermute | solution.py:193
  53.0 1.9 %collective-permute-start.1 = (s16[16,32,128]{2,1,0:T(8,128)(2,1)S(1)}, s16[16,32,128]{2,1,0:T(8,128)(2,1)S(1)}, u32[]{:S(2)}, u32[]{:S(2)}) collective-permute-start(s16[16,32,128]{2,1,0:T(8,128)(2,1)S(1)} %all_gather.6.both_ref), channel_id=1, source_target_pairs={{0,24},{1,49},{8,16},{9,57},{16,8},{17,33},{24,0},{25,41},{32,56},... | collective-permute-start | bytes 393224 | tf_op jit(solution)/shard_map/ppermute | solution.py:193
  54.9 4.8 %collective-permute-start = (s16[16,32,128]{2,1,0:T(8,128)(2,1)S(1)}, s16[16,32,128]{2,1,0:T(8,128)(2,1)S(1)}, u32[]{:S(2)}, u32[]{:S(2)}) collective-permute-start(s16[16,32,128]{2,1,0:T(8,128)(2,1)S(1)} %all_gather.6.both_ref), channel_id=1, source_target_pairs={{0,16},{1,57},{8,24},{9,49},{16,0},{17,41},{24,8},{25,33},{32,48},... | collective-permute-start | bytes 393224 | tf_op jit(solution)/shard_map/ppermute | solution.py:193
  59.7 0.3 select_convert_fusion.pick_ref
  60.0 0.0 collective-permute-done.3
  60.0 0.0 collective-permute-done.2
  60.0 2.4 %collective-permute-done.1 = s16[16,32,128]{2,1,0:T(8,128)(2,1)S(1)} collective-permute-done((s16[16,32,128]{2,1,0:T(8,128)(2,1)S(1)}, s16[16,32,128]{2,1,0:T(8,128)(2,1)S(1)}, u32[]{:S(2)}, u32[]{:S(2)}) %collective-permute-start.1) | collective-permute-done | bytes 131104 | tf_op jit(solution)/shard_map/ppermute | solution.py:193
  62.5 2.8 %collective-permute-done = s16[16,32,128]{2,1,0:T(8,128)(2,1)S(1)} collective-permute-done((s16[16,32,128]{2,1,0:T(8,128)(2,1)S(1)}, s16[16,32,128]{2,1,0:T(8,128)(2,1)S(1)}, u32[]{:S(2)}, u32[]{:S(2)}) %collective-permute-start) | collective-permute-done | bytes 131104 | tf_op jit(solution)/shard_map/ppermute | solution.py:193
  65.3 3.4 %all_gather.7.fetched_ref = s16[16,224,128]{2,1,0:T(8,128)(2,1)S(1)} all-gather(s16[16,112,128]{2,1,0:T(8,128)(2,1)S(1)} %pad_add_fusion), channel_id=1, replica_groups=mesh['row'=16,'y'=8,'xh'=4,'core'=2] {'core'}, dimensions={1}, use_global_device_ids=true | all-gather | bytes 1376256 | tf_op jit(solution)/shard_map/all_gather | solution.py:195
  68.7 0.0 all-to-all-done.tile_ref
  68.7 2.4 %shard_map.57 = bf16[2,112,2048]{2,1,0:T(8,128)(2,1)} custom-call(bf16[256,256]{1,0:T(8,128)(2,1)S(1)} %select_convert_fusion.pick_ref, s16[16,240,128]{2,1,0:T(8,128)(2,1)S(1)} %all-to-all-done.tile_ref, s16[16,32,128]{2,1,0:T(8,128)(2,1)S(1)} %all_gather.6.both_ref, s16[16,224,128]{2,1,0:T(8,128)(2,1)S(1)} %all_gather.7.fetched_ref), custom_call_target="tpu_custom_call" | custom-call | flops 700000000 | bytes 4000000 | tf_op jit(solution)/shard_map/pallas_call | solution.py:170
  (5 shorter events, 0.0 us)
Async XLA Ops:
  1.5 33.8 %all-to-all-start.1 = ((s16[64,4,128]{2,1,0:T(4,128)(2,1)}), s16[64,4,128]{2,1,0:T(4,128)(2,1)S(1)}, u32[]{:S(2)}, u32[]{:S(2)}) async-start(s16[64,4,128]{2,1,0:T(4,128)(2,1)} %bitcast.5), calls=%async_computation.1 | async-start | bytes 131072 | tf_op jit(solution)/shard_map/all_to_all | solution.py:200
  35.2 33.4 %all-to-all-start = ((s16[16,240,128]{2,1,0:T(8,128)(2,1)}), s16[16,240,128]{2,1,0:T(8,128)(2,1)S(1)}, u32[]{:S(2)}, u32[]{:S(2)}) async-start(s16[16,240,128]{2,1,0:T(8,128)(2,1)} %shard_map.55), calls=%async_computation | async-start | bytes 1966080 | tf_op jit(solution)/shard_map/all_to_all | solution.py:202
  38.9 21.1 %collective-permute-start.3 = (s16[16,16,128]{2,1,0:T(8,128)(2,1)S(1)}, s16[16,16,128]{2,1,0:T(8,128)(2,1)S(1)}, u32[]{:S(2)}, u32[]{:S(2)}) collective-permute-start(s16[16,16,128]{2,1,0:T(8,128)(2,1)S(1)} %bitcast.3), channel_id=1, source_target_pairs={{0,8},{8,0},{16,24},{24,16},{32,40},{40,32},{48,56},{56,48},{1,9},... | collective-permute-start | bytes 196616 | tf_op jit(solution)/shard_map/ppermute | solution.py:187
  46.2 13.8 %collective-permute-start.2 = (s16[16,32,128]{2,1,0:T(8,128)(2,1)S(1)}, s16[16,32,128]{2,1,0:T(8,128)(2,1)S(1)}, u32[]{:S(2)}, u32[]{:S(2)}) collective-permute-start(s16[16,32,128]{2,1,0:T(8,128)(2,1)S(1)} %all_gather.6.both_ref), channel_id=1, source_target_pairs={{0,32},{1,41},{8,40},{9,33},{16,48},{17,57},{24,56},{25,49},{32,0}... | collective-permute-start | bytes 393224 | tf_op jit(solution)/shard_map/ppermute | solution.py:193
  53.0 9.5 %collective-permute-start.1 = (s16[16,32,128]{2,1,0:T(8,128)(2,1)S(1)}, s16[16,32,128]{2,1,0:T(8,128)(2,1)S(1)}, u32[]{:S(2)}, u32[]{:S(2)}) collective-permute-start(s16[16,32,128]{2,1,0:T(8,128)(2,1)S(1)} %all_gather.6.both_ref), channel_id=1, source_target_pairs={{0,24},{1,49},{8,16},{9,57},{16,8},{17,33},{24,0},{25,41},{32,56},... | collective-permute-start | bytes 393224 | tf_op jit(solution)/shard_map/ppermute | solution.py:193
  54.9 10.4 %collective-permute-start = (s16[16,32,128]{2,1,0:T(8,128)(2,1)S(1)}, s16[16,32,128]{2,1,0:T(8,128)(2,1)S(1)}, u32[]{:S(2)}, u32[]{:S(2)}) collective-permute-start(s16[16,32,128]{2,1,0:T(8,128)(2,1)S(1)} %all_gather.6.both_ref), channel_id=1, source_target_pairs={{0,16},{1,57},{8,24},{9,49},{16,0},{17,41},{24,8},{25,33},{32,48},... | collective-permute-start | bytes 393224 | tf_op jit(solution)/shard_map/ppermute | solution.py:193
